TPU v7x, 256 devices: a whole 4x4x8 slice. The times are simulated.
256 devices in a mesh: dom: 64 (over z, y_hi, x), orb: 4 (over y_lo, core).
Axes of the slice: x: 4, y: 4 (y_hi: 2, y_lo: 2; y = y_hi * 2 + y_lo), z: 8, core: 2. Of those that a mesh axis runs over, the one named last changes fastest.
Arguments:
- orbitals: float32 [16, 1024, 16, 128], P('orb', 'dom'), may hold values from -12 to 12, as said below
- local_potential: float32 [1024, 16, 128], P('dom'), may hold values from -3 to 1
- sphere_index: int32 [1024, 128], P('dom'), may hold values from -1 to 32767, as said below
- projector: float32 [1024, 4, 128], P('dom'), may hold values from -1 to 1
- species: int32 [1024], P('dom'), may hold values from 0 to 2
- atom_count: int32 [64], P('dom'), may hold values from 1 to 16, as said below
- channel_energy: float32 [3, 4], replicated, may hold values from 0.5 to 4
Outputs:
- filtered: float32 [16, 1024, 16, 128], P('orb', 'dom')
- gram: float32 [16, 16], replicated
Inputs may be any that keep to these rules, and one draw needn't show every extreme that they name: `orbitals`: float entries; no further structure is promised. `sphere_index`: row a lists distinct cells of the slab of slot a, as flat indices (x * 16 + y) * 128 + z with x counted within the slab, followed by -1 entries as padding; a row holds 64 to 128 cells. `atom_count`: at most 16 live atoms on a slab; some slab holds exactly 16.
All inputs are finite; a program needn't handle non-finite values.
Results may differ from a plain program's by a relative error of at most 0.00011.
Values sent between devices are 32-bit elements; how exact they have to be, the bound alone decides.
No kernel may reach another device: no remote copies, remote signals or barrier semaphores. Data moves between devices by JAX's collectives and lax.ppermute only.
A program may use at most 128 MiB of HBM per device.

v0:
```python
import jax
import jax.numpy as jnp
from jax import lax
from jax.sharding import PartitionSpec as P

RADIUS = 6


STENCIL = (
    -5369.0 / 1800.0,
    12.0 / 7.0,
    -15.0 / 56.0,
    10.0 / 189.0,
    -1.0 / 112.0,
    2.0 / 1925.0,
    -1.0 / 16632.0,
)
LOWER_EDGE = 2.0
UPPER_EDGE = 17.0
HIGHEST = lax.Precision.HIGHEST


def padded_2(cells, sides, width):
    for axis, dim in sides:
        count = lax.axis_size(axis)
        head = lax.slice_in_dim(cells, 0, width, axis=dim)
        tail = lax.slice_in_dim(cells, cells.shape[dim] - width, cells.shape[dim], axis=dim)
        cells = jnp.concatenate(
            [
                lax.ppermute(tail, axis, [(i, (i + 1) % count) for i in range(count)]),
                cells,
                lax.ppermute(head, axis, [((i + 1) % count, i) for i in range(count)]),
            ],
            axis=dim,
        )
    return cells


def nonlocal_part(orb_block, safe_cells, in_sphere, projector, strength):
    orb_count = orb_block.shape[0]
    atom_slots, points = safe_cells.shape
    flat_block = orb_block.reshape(orb_count, -1)
    picked = jnp.take(flat_block, safe_cells.reshape(-1), axis=1).reshape(
        orb_count, atom_slots, points
    )
    picked = jnp.where(in_sphere[None], picked, 0.0)
    coefficient = jnp.einsum("apk,oak->oap", projector, picked, precision=HIGHEST)
    scaled = coefficient * strength[None]
    spread = jnp.einsum("apk,oap->oak", projector, scaled, precision=HIGHEST)
    spread = jnp.where(in_sphere[None], spread, 0.0)
    accumulated = (
        jnp.zeros_like(flat_block).at[:, safe_cells.reshape(-1)].add(spread.reshape(orb_count, -1))
    )
    return accumulated.reshape(orb_block.shape)


def laplace_rows(padded, first, count):
    centre = padded[:, first : first + count]
    lap_total = 3.0 * STENCIL[0] * centre
    for offset in range(1, RADIUS + 1):
        below_rows = padded[:, first - offset : first - offset + count]
        above_rows = padded[:, first + offset : first + offset + count]
        neighbours = below_rows + above_rows
        neighbours = neighbours + jnp.roll(centre, offset, 2) + jnp.roll(centre, -offset, 2)
        neighbours = neighbours + jnp.roll(centre, offset, 3) + jnp.roll(centre, -offset, 3)
        lap_total = lap_total + STENCIL[offset] * neighbours
    return lap_total


def apply_operator(orb_block, potential, safe_cells, in_sphere, projector, strength):
    slab_cells = orb_block.shape[1]
    padded = padded_2(orb_block, (("dom", 1),), RADIUS)
    lap_total = laplace_rows(padded, RADIUS, slab_cells)
    return (
        -0.5 * lap_total
        + potential[None] * orb_block
        + nonlocal_part(orb_block, safe_cells, in_sphere, projector, strength)
    )


def gram_terms(orb_block):
    flat_rows = orb_block.reshape(orb_block.shape[0], -1)
    return lax.dot_general(
        flat_rows,
        flat_rows,
        (((1,), (1,)), ((), ())),
        precision=HIGHEST,
        preferred_element_type=jnp.float32,
    )


def on_device(
    orbitals, local_potential, sphere_index, projector, species, atom_count, channel_energy
):
    kind_count = channel_energy.shape[0]
    onehot = (species[:, None] == jnp.arange(kind_count, dtype=jnp.int32)[None, :]).astype(
        jnp.float32
    )
    is_live = jnp.arange(species.shape[0], dtype=jnp.int32) < atom_count[0]
    strength = jnp.where(is_live[:, None], jnp.dot(onehot, channel_energy, precision=HIGHEST), 0.0)
    in_sphere = sphere_index >= 0
    safe_cells = jnp.where(in_sphere, sphere_index, 0)
    mid_point = 0.5 * (UPPER_EDGE + LOWER_EDGE)
    half_width = 0.5 * (UPPER_EDGE - LOWER_EDGE)
    step_one = (
        apply_operator(orbitals, local_potential, safe_cells, in_sphere, projector, strength)
        - mid_point * orbitals
    ) / half_width
    step_two = (
        2.0
        * (
            apply_operator(step_one, local_potential, safe_cells, in_sphere, projector, strength)
            - mid_point * step_one
        )
        / half_width
        - orbitals
    )
    gathered = lax.all_gather(step_two, "orb", axis=0, tiled=True)
    summed = lax.psum(gram_terms(gathered), "dom")
    cell_total = step_two.shape[1] * step_two.shape[2] * step_two.shape[3] * lax.axis_size("dom")
    return (step_two, summed / cell_total)


def solution(mesh):
    placed = (
        P("orb", "dom", None, None),
        P("dom", None, None),
        P("dom", None),
        P("dom", None, None),
        P("dom"),
        P("dom"),
        P(),
    )
    return jax.shard_map(
        on_device,
        mesh=mesh,
        in_specs=placed,
        out_specs=(P("orb", "dom", None, None), P()),
        check_vma=False,
    )
```

profile of v0, /device:TPU:8, one launch (start us, length us, event | category | flops | bytes accessed | tf_op | source)
XLA Modules:
  0.0 443.9 jit_solution(2502118027221147633)
XLA Ops:
  7.2 1.8 fusion.167
  9.1 1.5 collective-permute-start
  10.6 8.3 %collective-permute-start.1 = (f32[4,6,16,128]{3,2,1,0:T(8,128)}, f32[4,6,16,128]{3,2,1,0:T(8,128)S(1)}, u32[]{:S(2)}, u32[]{:S(2)}) collective-permute-start(f32[4,6,16,128]{3,2,1,0:T(8,128)} %get-tuple-element.102), channel_id=1, source_target_pairs={{4,0},{8,4},{12,8},{16,12},{20,16},{24,20},{28,24},{32,28},{36,32}... | collective-permute-start | bytes 589832 | tf_op jit(solution)/shard_map/ppermute | solution.py:32
  20.3 9.7 %copy.134 = f32[4,16,16,128]{0,3,2,1:T(8,128)} copy(f32[4,16,16,128]{3,2,1,0:T(8,128)} %param.9) | data formatting | bytes 1048576 | tf_op args[0]
  31.3 1.1 fusion.171
  33.5 1.1 fusion.149
  34.6 1.1 fusion.150
  36.8 1.2 fusion.153
  40.1 1.2 fusion.157
  43.5 1.2 fusion.161
  44.7 1.2 fusion.162
  48.1 1.2 fusion.166
  53.6 13.4 %gather_fusion = f32[2048,4]{1,0:T(8,128)} fusion(f32[4,32768]{0,1:T(8,128)} %bitcast.49, s32[2048]{0:T(1024)S(1)} %fusion.117), kind=kCustom, calls=%fused_computation.clone | custom fusion | bytes 73728 | tf_op jit(solution)/shard_map/jit(_take)/gather | solution.py:43
  67.0 1.6 broadcast_select_fusion.1
  71.4 19.1 %scatter_custom_fusion = f32[4,32768]{0,1:T(8,128)} fusion(s32[2048]{0:T(1024)} %bitcast.54, f32[2048,4]{1,0:T(8,128)S(1)} %copy.137, f32[]{:T(128)} %constant.14.clone.1), kind=kCustom, calls=%fused_computation.6 | custom fusion | flops 8192 | bytes 524800 | tf_op jit(solution)/shard_map/scatter-add | solution.py:52
  90.5 10.0 %copy.146 = f32[4,16,16,128]{3,2,1,0:T(8,128)S(1)} copy(f32[4,16,16,128]{0,3,2,1:T(8,128)} %bitcast.48) | data formatting | bytes 1048576 | tf_op jit(solution)/shard_map/reshape | solution.py:54
  101.3 8.8 %broadcast_multiply_fusion = (f32[4,16,16,128]{3,2,1,0:T(8,128)S(1)}, f32[4,16,16,128]{3,2,1,0:T(8,128)S(1)}) fusion(f32[4,16,16,128]{3,2,1,0:T(8,128)S(1)} %copy-done.1, f32[4,16,16,128]{3,2,1,0:T(8,128)S(1)} %copy.146, f32[16,16,128]{2,1,0:T(8,128)} %param.10, f32[4,16,16,6]{3,2,1,0:T(8,128)} %get-tuple-element.108, ...), kind=kLoop, calls=%fused_computation.148 | loop fusion | flops 9699328 | bytes 21102592 | tf_op jit(solution)/shard_map/div | solution.py:105
  110.2 8.7 %copy.147 = f32[4,16,16,128]{0,3,2,1:T(8,128)} copy(f32[4,16,16,128]{3,2,1,0:T(8,128)S(1)} %get-tuple-element.7) | data formatting | bytes 1048576 | tf_op jit(solution)/shard_map/reshape | solution.py:42
  122.0 1.1 fusion.126
  125.3 1.2 fusion.130
  135.3 1.1 fusion.142
  143.1 13.4 %gather_fusion.1 = f32[2048,4]{1,0:T(8,128)} fusion(f32[4,32768]{0,1:T(8,128)} %bitcast.50, s32[2048]{0:T(1024)S(1)} %fusion.117), kind=kCustom, calls=%fused_computation.1.clone | custom fusion | bytes 73728 | tf_op jit(solution)/shard_map/jit(_take)/gather | solution.py:43
  156.5 1.6 broadcast_select_fusion
  160.2 1.4 copy.141
  161.6 19.3 %scatter_custom_fusion.1 = f32[4,32768]{0,1:T(8,128)} fusion(s32[2048]{0:T(1024)} %bitcast.55, f32[2048,4]{1,0:T(8,128)} %copy.141, f32[]{:T(128)} %constant.14.clone.1), kind=kCustom, calls=%fused_computation.4 | custom fusion | flops 8192 | bytes 524800 | tf_op jit(solution)/shard_map/scatter-add | solution.py:52
  181.0 10.0 %copy.148 = f32[4,16,16,128]{3,2,1,0:T(8,128)S(1)} copy(f32[4,16,16,128]{0,3,2,1:T(8,128)} %bitcast.47) | data formatting | bytes 1048576 | tf_op jit(solution)/shard_map/reshape | solution.py:54
  191.3 7.7 %collective-permute-start.3 = (f32[4,6,16,128]{3,2,1,0:T(8,128)}, f32[4,6,16,128]{3,2,1,0:T(8,128)S(1)}, u32[]{:S(2)}, u32[]{:S(2)}) collective-permute-start(f32[4,6,16,128]{3,2,1,0:T(8,128)} %get-tuple-element.58), channel_id=1, source_target_pairs={{4,0},{8,4},{12,8},{16,12},{20,16},{24,20},{28,24},{32,28},{36,32}... | collective-permute-start | bytes 589832 | tf_op jit(solution)/shard_map/ppermute | solution.py:32
  199.1 4.5 %collective-permute-done.2 = f32[4,6,16,128]{3,2,1,0:T(8,128)S(1)} collective-permute-done((f32[4,6,16,128]{3,2,1,0:T(8,128)}, f32[4,6,16,128]{3,2,1,0:T(8,128)S(1)}, u32[]{:S(2)}, u32[]{:S(2)}) %collective-permute-start.2) | collective-permute-done | bytes 196640 | tf_op jit(solution)/shard_map/ppermute | solution.py:30
  203.6 9.1 %fusion.27 = f32[4,16,16,128]{3,2,1,0:T(8,128)} fusion(f32[4,16,16,128]{3,2,1,0:T(8,128)S(1)} %copy-done.1, f32[4,16,16,128]{3,2,1,0:T(8,128)S(1)} %copy.148, f32[4,16,16,128]{3,2,1,0:T(8,128)S(1)} %get-tuple-element.7, f32[4,6,16,128]{3,2,1,0:T(8,128)S(1)} %collective-permute-done.3, f32[4,6,16,128]{3,2,1,0:T(8,128)S(1)} %collective-permute-done.2, ...), kind=kLoop, calls=%fused_computation.54 | loop fusion | flops 11403264 | bytes 15728640 | tf_op jit(solution)/shard_map/sub | solution.py:110
  212.7 30.5 %all-gather.2.cloned.1.call-done = f32[16,16,16,128]{3,2,1,0:T(8,128)} async-done(((f32[4,16,16,128]{3,2,1,0:T(8,128)}), f32[16,16,16,128]{3,2,1,0:T(8,128)}) %all-gather.2.cloned.1.call-update) | async-done | bytes 2097168 | tf_op jit(solution)/shard_map/all_gather | solution.py:118
  243.2 6.9 %fusion.10 = f32[16,16]{1,0:T(8,128)S(1)} fusion(f32[16,16,16,128]{3,2,1,0:T(8,128)} %all-gather.2.cloned.1.call-done), kind=kOutput, calls=%fused_computation.28 | convolution fusion | flops 100663296 | bytes 2098176 | tf_op jit(solution)/shard_map/dot_general | solution.py:83
  250.1 186.3 %psum.7 = f32[16,16]{1,0:T(8,128)S(1)} all-reduce(f32[16,16]{1,0:T(8,128)S(1)} %fusion.10), channel_id=1, replica_groups=mesh['dom'=64,'orb'=4] {'dom'}, use_global_device_ids=true, to_apply=%region_2.4 | all-reduce | flops 256 | bytes 2048 | tf_op jit(solution)/shard_map/psum | solution.py:119
  (84 shorter events, 42.5 us)
Async XLA Ops:
  7.2 62.7 %copy-start = (f32[16,4,128]{2,1,0:T(4,128)S(1)}, f32[16,4,128]{2,1,0:T(4,128)}, u32[]{:S(2)}) copy-start(f32[16,4,128]{2,1,0:T(4,128)} %param.12) | copy-start | bytes 98308
  7.2 22.9 %copy-start.1 = (f32[4,16,16,128]{3,2,1,0:T(8,128)S(1)}, f32[4,16,16,128]{3,2,1,0:T(8,128)}, u32[]{:S(2)}) copy-start(f32[4,16,16,128]{3,2,1,0:T(8,128)} %param.9) | copy-start | bytes 1572868
  7.2 22.9 %copy-start.4 = (s32[16,128]{1,0:T(8,128)S(1)}, s32[16,128]{1,0:T(8,128)}, u32[]{:S(2)}) copy-start(s32[16,128]{1,0:T(8,128)} %param.11) | copy-start | bytes 24580
  7.2 236.0 %all-gather.2.cloned.1.call-start = ((), (), s32[]{:S(2)}) async-start(), calls=%async_computation | async-start | bytes 2621440 | tf_op jit(solution)/shard_map/all_gather | solution.py:118
  9.1 92.1 %collective-permute-start = (f32[4,6,16,128]{3,2,1,0:T(8,128)}, f32[4,6,16,128]{3,2,1,0:T(8,128)S(1)}, u32[]{:S(2)}, u32[]{:S(2)}) collective-permute-start(f32[4,6,16,128]{3,2,1,0:T(8,128)} %get-tuple-element.101), channel_id=1, source_target_pairs={{0,4},{4,8},{8,12},{12,16},{16,20},{20,24},{24,28},{28,32},{32,36}... | collective-permute-start | bytes 589832 | tf_op jit(solution)/shard_map/ppermute | solution.py:30
  10.6 90.7 %collective-permute-start.1 = (f32[4,6,16,128]{3,2,1,0:T(8,128)}, f32[4,6,16,128]{3,2,1,0:T(8,128)S(1)}, u32[]{:S(2)}, u32[]{:S(2)}) collective-permute-start(f32[4,6,16,128]{3,2,1,0:T(8,128)} %get-tuple-element.102), channel_id=1, source_target_pairs={{4,0},{8,4},{12,8},{16,12},{20,16},{24,20},{28,24},{32,28},{36,32}... | collective-permute-start | bytes 589832 | tf_op jit(solution)/shard_map/ppermute | solution.py:32
  19.6 50.6 %copy-start.5 = (pred[16,128]{1,0:T(8,128)(4,1)}, pred[16,128]{1,0:T(8,128)(4,1)S(1)}, u32[]{:S(2)}) copy-start(pred[16,128]{1,0:T(8,128)(4,1)S(1)} %broadcast_compare_fusion) | copy-start | bytes 6148
  30.1 37.0 %copy-start.6 = (pred[2048]{0:T(1024)(128)(4,1)}, pred[2048]{0:T(1024)(128)(4,1)S(1)}, u32[]{:S(2)}) copy-start(pred[2048]{0:T(1024)(128)(4,1)S(1)} %compare_and_fusion) | copy-start | bytes 6148
  34.6 35.0 %copy-start.8 = (f32[3,4]{1,0:T(4,128)S(1)}, f32[3,4]{1,0:T(4,128)}, u32[]{:S(2)}) copy-start(f32[3,4]{1,0:T(4,128)} %param.15) | copy-start | bytes 148
  34.6 35.0 %copy-start.9 = (s32[16]{0:T(128)S(1)}, s32[16]{0:T(128)}, u32[]{:S(2)}) copy-start(s32[16]{0:T(128)} %param.13) | copy-start | bytes 196
  71.4 29.1 %copy-start.3 = (f32[16,16,128]{2,1,0:T(8,128)S(1)}, f32[16,16,128]{2,1,0:T(8,128)}, u32[]{:S(2)}) copy-start(f32[16,16,128]{2,1,0:T(8,128)} %param.10) | copy-start | bytes 393220
  123.1 33.3 %copy-start.7 = (pred[2048]{0:T(1024)(128)(4,1)S(1)}, pred[2048]{0:T(1024)(128)(4,1)}, u32[]{:S(2)}) copy-start(pred[2048]{0:T(1024)(128)(4,1)} %copy-done.6) | copy-start | bytes 6148
  161.6 41.9 %copy-start.2 = (f32[4,16,16,122]{3,2,1,0:T(8,128)S(1)}, f32[4,16,16,122]{3,2,1,0:T(8,128)}, u32[]{:S(2)}) copy-start(f32[4,16,16,122]{3,2,1,0:T(8,128)} %get-tuple-element.10) | copy-start | bytes 1499140
  191.0 12.6 %collective-permute-start.2 = (f32[4,6,16,128]{3,2,1,0:T(8,128)}, f32[4,6,16,128]{3,2,1,0:T(8,128)S(1)}, u32[]{:S(2)}, u32[]{:S(2)}) collective-permute-start(f32[4,6,16,128]{3,2,1,0:T(8,128)} %get-tuple-element.57), channel_id=1, source_target_pairs={{0,4},{4,8},{8,12},{12,16},{16,20},{20,24},{24,28},{28,32},{32,36}... | collective-permute-start | bytes 589832 | tf_op jit(solution)/shard_map/ppermute | solution.py:30
  191.3 12.3 %collective-permute-start.3 = (f32[4,6,16,128]{3,2,1,0:T(8,128)}, f32[4,6,16,128]{3,2,1,0:T(8,128)S(1)}, u32[]{:S(2)}, u32[]{:S(2)}) collective-permute-start(f32[4,6,16,128]{3,2,1,0:T(8,128)} %get-tuple-element.58), channel_id=1, source_target_pairs={{4,0},{8,4},{12,8},{16,12},{20,16},{24,20},{28,24},{32,28},{36,32}... | collective-permute-start | bytes 589832 | tf_op jit(solution)/shard_map/ppermute | solution.py:32
Sparse Core Ops, SparseCore 0:
  212.8 30.3 all-gather.1
where the time goes:
time: 445 us; the launch traced here: 444 us
  blocking collectives  186 us (42%)
  local copies, waits for them, and re-layouts  117 us (26%)
  other arithmetic  62.8 us (14%)
  waiting for transfers between devices  35 us (8%)
  starting transfers between devices  17.9 us (4%)
  between operations  14.9 us (3%)
  matrix products  9.49 us (2%)
    psum x1, blocking collectives, on_device(): summed = lax.psum(gram_terms(gathered), 'dom')  186 us
    scatter-add x2, other arithmetic, nonlocal_part(): jnp.zeros_like(flat_block).at[:, safe_cells.reshape(-1)]  38.4 us
    all_gather x1, waiting for transfers between devices, on_device(): gathered = lax.all_gather(step_two, 'orb', axis=0, tiled=True)  30.5 us
    gather x2, local copies, waits for them, and re-layouts, nonlocal_part(): jnp.take(flat_block, safe_cells.reshape(-1), axis=1)  26.7 us
    reshape x2, local copies, waits for them, and re-layouts, nonlocal_part(): return accumulated.reshape(orb_block.shape)  20 us
    ppermute x2, starting transfers between devices, padded_2(): lax.ppermute(head, axis, [((i + 1) % count, i) for i in range(count)])  16 us
    slice x12, local copies, waits for them, and re-layouts, laplace_rows(): jnp.roll(centre, offset, 3)  13.7 us
    slice x12, local copies, waits for them, and re-layouts, laplace_rows(): jnp.roll(centre, -offset, 3)  13.4 us
  transfers between devices with their start and end apart: 5, of which 2 were waited for; matrix products, arithmetic and copies ran while one was open for 18% of the time, Pallas kernels for 0%

commit v1 on v0

v1 whole, which is shorter than its diff:
```python
import functools

import jax
import jax.numpy as jnp
from jax import lax
from jax.experimental import pallas as pl
from jax.experimental.pallas import tpu as pltpu
from jax.sharding import PartitionSpec as P

RADIUS = 6
STENCIL = (
    -5369.0 / 1800.0,
    12.0 / 7.0,
    -15.0 / 56.0,
    10.0 / 189.0,
    -1.0 / 112.0,
    2.0 / 1925.0,
    -1.0 / 16632.0,
)
LOWER_EDGE = 2.0
UPPER_EDGE = 17.0
MID_POINT = 0.5 * (UPPER_EDGE + LOWER_EDGE)
HALF_WIDTH = 0.5 * (UPPER_EDGE - LOWER_EDGE)
VMEM = pltpu.VMEM
SMEM = pltpu.SMEM
NT = (((1,), (1,)), ((), ()))


def split(values):
    high = values.astype(jnp.bfloat16)
    return high, (values - high.astype(jnp.float32)).astype(jnp.bfloat16)


def nonlocal_rows(
    load_rows, orbs, index, projector, species, count, energy, parts, rowhot, zhot, picked, spread
):
    rows, lanes = 256, 128
    atoms, channels = projector.shape[0], projector.shape[1]
    for o in range(orbs):
        high, low = split(load_rows(o).T)
        parts[0, o * lanes : (o + 1) * lanes, :] = high
        parts[1, o * lanes : (o + 1) * lanes, :] = low
    cells = index[...]
    row_of = cells >> 7
    lane_of = cells & 127
    row_iota = lax.broadcasted_iota(jnp.int32, (rows, lanes), 0)
    lane_iota = lax.broadcasted_iota(jnp.int32, (lanes, lanes), 0)
    for a in range(atoms):
        at = slice(a * lanes, (a + 1) * lanes)
        rowhot[:, at] = jnp.where(row_iota == row_of[a : a + 1], 1.0, 0.0).astype(jnp.bfloat16)
    for a in range(0, atoms, 2):
        at = slice(a * lanes, (a + 2) * lanes)
        found = jnp.dot(parts[0], rowhot[:, at], preferred_element_type=jnp.float32)
        found = found + jnp.dot(parts[1], rowhot[:, at], preferred_element_type=jnp.float32)
        for b in range(2):
            hot = lane_iota == lane_of[a + b : a + b + 1]
            zhot[:, (a + b) * lanes : (a + b + 1) * lanes] = jnp.where(hot, 1.0, 0.0).astype(
                jnp.bfloat16
            )
            for o in range(orbs):
                block = found[o * lanes : (o + 1) * lanes, b * lanes : (b + 1) * lanes]
                picked[o, a + b : a + b + 1, :] = jnp.sum(
                    jnp.where(hot, block, 0.0), axis=0, keepdims=True
                )
    slot = lax.broadcasted_iota(jnp.int32, (atoms, 1), 0)
    live = slot < count[0]
    inside = cells >= 0
    total = [jnp.zeros((atoms, lanes), jnp.float32) for _ in range(orbs)]
    for p in range(channels):
        strength = jnp.zeros((atoms, 1), jnp.float32)
        for a in range(atoms):
            strength = jnp.where(slot == a, energy[species[a], p], strength)
        strength = jnp.where(live, strength, 0.0)
        shape = projector[:, p, :]
        for o in range(orbs):
            coefficient = jnp.sum(shape * picked[o], axis=1, keepdims=True)
            total[o] = total[o] + shape * (coefficient * strength)
    for o in range(orbs):
        high, low = split(jnp.where(inside, total[o], 0.0))
        for a in range(atoms):
            at = slice(a * lanes, (a + 1) * lanes)
            hot = zhot[:, at]
            spread[0, o * lanes : (o + 1) * lanes, at] = hot * high[a : a + 1]
            spread[1, o * lanes : (o + 1) * lanes, at] = hot * low[a : a + 1]
    out = lax.dot_general(rowhot[...], spread[0], NT, preferred_element_type=jnp.float32)
    return out + lax.dot_general(rowhot[...], spread[1], NT, preferred_element_type=jnp.float32)


def local_layer(load, potential, i, layers):
    centre = load(i)
    total = (potential - (1.5 * STENCIL[0] + MID_POINT)) * centre
    for k in range(1, RADIUS + 1):
        near = pltpu.roll(centre, k, 0) + pltpu.roll(centre, centre.shape[0] - k, 0)
        near = near + pltpu.roll(centre, k, 1) + pltpu.roll(centre, centre.shape[1] - k, 1)
        if i - k >= 0:
            near = near + load(i - k)
        if i + k < layers:
            near = near + load(i + k)
        total = total - (0.5 * STENCIL[k]) * near
    return total


def first_kernel(
    species, count, energy, v, potential, index, projector, out, parts, rowhot, zhot, picked, spread
):
    orbs, layers = v.shape[0], v.shape[1]
    hat = nonlocal_rows(
        lambda o: v[o].reshape(256, 128),
        orbs,
        index,
        projector,
        species,
        count,
        energy,
        parts,
        rowhot,
        zhot,
        picked,
        spread,
    )
    for o in range(orbs):
        for i in range(layers):
            total = local_layer(lambda j: v[o, j], potential[i], i, layers)
            total = total + hat[i * 16 : (i + 1) * 16, o * 128 : (o + 1) * 128]
            out[o, i] = total * (1.0 / HALF_WIDTH)


def second_kernel(
    species,
    count,
    energy,
    v,
    potential,
    index,
    projector,
    low,
    middle,
    high,
    out,
    parts,
    rowhot,
    zhot,
    picked,
    spread,
    held,
):
    orbs, layers = v.shape[0], v.shape[1]
    held[:, :RADIUS] = low[...]
    held[:, RADIUS : layers - RADIUS] = middle[:, RADIUS : layers - RADIUS]
    held[:, layers - RADIUS :] = high[...]
    hat = nonlocal_rows(
        lambda o: held[o].reshape(256, 128),
        orbs,
        index,
        projector,
        species,
        count,
        energy,
        parts,
        rowhot,
        zhot,
        picked,
        spread,
    )
    for o in range(orbs):
        for i in range(layers):
            total = local_layer(lambda j: held[o, j], potential[i], i, layers)
            total = total + hat[i * 16 : (i + 1) * 16, o * 128 : (o + 1) * 128]
            out[o, i] = total * (2.0 / HALF_WIDTH) - v[o, i]


def from_below(below, o, i):
    total = STENCIL[i + 1] * below[o, RADIUS - 1]
    for k in range(i + 2, RADIUS + 1):
        total = total + STENCIL[k] * below[o, RADIUS + i - k]
    return total


def from_above(above, o, j):
    total = STENCIL[j + 1] * above[o, 0]
    for k in range(j + 2, RADIUS + 1):
        total = total + STENCIL[k] * above[o, k - j - 1]
    return total


def first_edges(part, below, above, low, high):
    orbs, layers = part.shape[0], part.shape[1]
    scale = -0.5 / HALF_WIDTH
    for o in range(orbs):
        for i in range(RADIUS):
            low[o, i] = part[o, i] + scale * from_below(below, o, i)
            high[o, RADIUS - 1 - i] = part[o, layers - 1 - i] + scale * from_above(above, o, i)


def second_edges(me, part, below, above, out, own, send_1, send_2, send_3):
    orbs, layers = part.shape[0], part.shape[1]
    scale = -1.0 / HALF_WIDTH
    out[:, RADIUS : layers - RADIUS] = part[:, RADIUS : layers - RADIUS]
    for o in range(orbs):
        for i in range(RADIUS):
            out[o, i] = part[o, i] + scale * from_below(below, o, i)
            out[o, layers - 1 - i] = part[o, layers - 1 - i] + scale * from_above(above, o, i)
    depth = own.shape[1]
    for k, chunk in enumerate((own, send_1, send_2, send_3)):
        first = pl.multiple_of((me[0] ^ k) * depth, depth)
        for o in range(orbs):
            chunk[o] = out[o, pl.ds(first, depth)]


def gram_kernel(me, own, got_1, got_2, got_3, out, rows):
    orbs, depth = own.shape[0], own.shape[1]
    for k, chunk in enumerate((own, got_1, got_2, got_3)):
        first = (me[0] ^ k) * orbs
        for o in range(orbs):
            for x in range(depth):
                rows[x, first + o] = chunk[o, x]
    total = jnp.zeros((256, 256), jnp.float32)
    for x in range(depth):
        high, low = split(rows[x].reshape(256, 128))
        left = jnp.concatenate([high, high, low], axis=1)
        right = jnp.concatenate([high, low, high], axis=1)
        total = total + lax.dot_general(left, right, NT, preferred_element_type=jnp.float32)
    same = (lax.broadcasted_iota(jnp.int32, (256, 256), 0) & 15) == (
        lax.broadcasted_iota(jnp.int32, (256, 256), 1) & 15
    )
    total = jnp.where(same, total, 0.0)
    total = jnp.sum(total.reshape(16, 16, 256), axis=1)
    lane = lax.broadcasted_iota(jnp.int32, (256, 128), 1)
    place = (lane & 15) == (lax.broadcasted_iota(jnp.int32, (256, 128), 0) >> 4)
    place = jnp.where(place, 1.0, 0.0)
    spread = jnp.dot(
        total, place, precision=lax.Precision.HIGHEST, preferred_element_type=jnp.float32
    )
    keep = (lax.broadcasted_iota(jnp.int32, (16, 128), 1) >> 4) == (
        lax.broadcasted_iota(jnp.int32, (16, 128), 0) & 7
    )
    spread = jnp.where(keep, spread, 0.0)
    packed = jnp.sum(spread.reshape(2, 8, 128), axis=1)
    out[...] = jnp.broadcast_to(packed[None], out.shape)


def final_kernel(cells, terms, out):
    packed = jnp.sum(terms[...], axis=0)
    row = lax.broadcasted_iota(jnp.int32, (16, 128), 0)
    lane = lax.broadcasted_iota(jnp.int32, (16, 128), 1)
    spread = jnp.where(row < 8, packed[0:1], packed[1:2])
    spread = jnp.where((lane >> 4) == (row & 7), spread, 0.0)
    place = (lax.broadcasted_iota(jnp.int32, (128, 16), 0) & 15) == lax.broadcasted_iota(
        jnp.int32, (128, 16), 1
    )
    place = jnp.where(place, 1.0, 0.0)
    total = jnp.dot(
        spread, place, precision=lax.Precision.HIGHEST, preferred_element_type=jnp.float32
    )
    out[...] = total * (1.0 / cells)


def call(kernel, outs, in_specs, scratch=(), flops=10_000_000, limit=48 * 2**20):
    return pl.pallas_call(
        kernel,
        out_shape=outs,
        in_specs=in_specs,
        out_specs=jax.tree.map(lambda _: pl.BlockSpec(memory_space=VMEM), outs),
        scratch_shapes=list(scratch),
        compiler_params=pltpu.CompilerParams(vmem_limit_bytes=limit),
        cost_estimate=pl.CostEstimate(flops=flops, bytes_accessed=2**21, transcendentals=0),
    )


def on_device(
    orbitals, local_potential, sphere_index, projector, species, atom_count, channel_energy
):
    f32 = jnp.float32
    in_vmem = pl.BlockSpec(memory_space=VMEM)
    in_smem = pl.BlockSpec(memory_space=SMEM)
    orbs, layers, wide, deep = orbitals.shape
    doms, orb_devices = lax.axis_size("dom"), lax.axis_size("orb")
    up = [(i, (i + 1) % doms) for i in range(doms)]
    down = [((i + 1) % doms, i) for i in range(doms)]
    me = lax.axis_index("orb").astype(jnp.int32).reshape(1)
    edge = jax.ShapeDtypeStruct((orbs, RADIUS, wide, deep), f32)
    block = jax.ShapeDtypeStruct(orbitals.shape, f32)
    points = sphere_index.shape[0] * sphere_index.shape[1]
    scratch = [
        pltpu.VMEM((2, orbs * deep, layers * wide), jnp.bfloat16),
        pltpu.VMEM((layers * wide, points), jnp.bfloat16),
        pltpu.VMEM((deep, points), jnp.bfloat16),
        pltpu.VMEM((orbs,) + sphere_index.shape, f32),
        pltpu.VMEM((2, orbs * deep, points), jnp.bfloat16),
    ]
    scalars = (species, atom_count, channel_energy)
    fields = (orbitals, local_potential, sphere_index, projector)

    below = lax.ppermute(orbitals[:, layers - RADIUS :], "dom", up)
    above = lax.ppermute(orbitals[:, :RADIUS], "dom", down)
    part = call(
        first_kernel, block, [in_smem] * 3 + [in_vmem] * 4, scratch, flops=3_000_000_000
    )(*scalars, *fields)
    low, high = call(first_edges, (edge, edge), [in_vmem] * 3)(part, below, above)

    below = lax.ppermute(high, "dom", up)
    above = lax.ppermute(low, "dom", down)
    part = call(
        second_kernel,
        block,
        [in_smem] * 3 + [in_vmem] * 7,
        scratch + [pltpu.VMEM(orbitals.shape, f32)],
        flops=3_000_000_000,
    )(*scalars, *fields, low, part, high)
    quarter = jax.ShapeDtypeStruct((orbs, layers // orb_devices, wide, deep), f32)
    filtered, own, *sends = call(
        second_edges, (block,) + (quarter,) * 4, [in_smem] + [in_vmem] * 3
    )(me, part, below, above)

    got = [
        lax.ppermute(sends[k - 1], "orb", [(i, i ^ k) for i in range(orb_devices)])
        for k in (1, 2, 3)
    ]
    everyone = doms * orb_devices
    terms = call(
        gram_kernel,
        jax.ShapeDtypeStruct((everyone, 2, 128), f32),
        [in_smem] + [in_vmem] * 4,
        [pltpu.VMEM((layers // orb_devices, orbs * orb_devices, wide, deep), f32)],
    )(me, own, *got)
    terms = lax.all_to_all(terms, ("dom", "orb"), 0, 0)
    gram = call(
        functools.partial(final_kernel, float(layers * wide * deep * doms)),
        jax.ShapeDtypeStruct((16, 16), f32),
        [in_vmem],
    )(terms)
    return filtered, gram


def solution(mesh):
    placed = (
        P("orb", "dom", None, None),
        P("dom", None, None),
        P("dom", None),
        P("dom", None, None),
        P("dom"),
        P("dom"),
        P(),
    )
    return jax.shard_map(
        on_device,
        mesh=mesh,
        in_specs=placed,
        out_specs=(P("orb", "dom", None, None), P()),
        check_vma=False,
    )
```

time: 445 us -> 70.2 us (0.16)
  the two profiles are of different devices: /device:TPU:8 before, /device:TPU:1 now
where the time goes in v1:
time: 70.2 us; the launch traced here: 70.1 us
  blocking collectives  20.8 us (30%)
  waiting for transfers between devices  18.5 us (26%)
  starting transfers between devices  17 us (24%)
  Pallas kernels  11.2 us (16%)
  between operations  1.44 us (2%)
  local copies, waits for them, and re-layouts  1.14 us (2%)
    all_to_all x1, blocking collectives, on_device(): terms = lax.all_to_all(terms, ('dom', 'orb'), 0, 0)  20.8 us
    ppermute x1, starting transfers between devices, on_device(): above = lax.ppermute(orbitals[:, :RADIUS], 'dom', down)  11.3 us
    ppermute x3, waiting for transfers between devices, on_device(): lax.ppermute(sends[k - 1], 'orb', [(i, i ^ k) for i in range(orb_devices)])  6.4 us
    ppermute x1, waiting for transfers between devices, on_device(): below = lax.ppermute(orbitals[:, layers - RADIUS:], 'dom', up)  6.33 us
    ppermute x1, waiting for transfers between devices, on_device(): below = lax.ppermute(high, 'dom', up)  5.79 us
    pallas_call x1, Pallas kernels, on_device(): call(second_kernel, block, [in_smem] * 3 + [in_vmem] * 7, scratch + [pltp...  4.19 us
    ppermute x3, starting transfers between devices, on_device(): lax.ppermute(sends[k - 1], 'orb', [(i, i ^ k) for i in range(orb_devices)])  4.18 us
    pallas_call x1, Pallas kernels, on_device(): call(first_kernel, block, [in_smem] * 3 + [in_vmem] * 4, scratch, flops=3...  4.08 us
  transfers between devices with their start and end apart: 7, of which 4 were waited for; matrix products, arithmetic and copies ran while one was open for 0% of the time, Pallas kernels for 12%

profile of v1, /device:TPU:1, one launch (start us, length us, event | category | flops | bytes accessed | tf_op | source)
XLA Modules:
  0.0 70.1 jit_solution(11362559647657534475)
XLA Ops:
  0.6 0.0 copy-start
  0.6 0.0 copy-start.2
  0.6 0.0 copy-start.1
  0.7 1.1 %fusion = (f32[4,6,16,128]{3,2,1,0:T(8,128)S(1)}, f32[4,6,16,128]{3,2,1,0:T(8,128)S(1)}) fusion(f32[4,16,16,128]{3,2,1,0:T(8,128)} %v.3), kind=kLoop, calls=%fused_computation | loop fusion | bytes 786432 | tf_op jit(solution)/shard_map/slice | solution.py:295
  1.8 0.0 copy-start.3
  1.8 11.3 %collective-permute-start.1 = (f32[4,6,16,128]{3,2,1,0:T(8,128)S(1)}, f32[4,6,16,128]{3,2,1,0:T(8,128)S(1)}, u32[]{:S(2)}, u32[]{:S(2)}) collective-permute-start(f32[4,6,16,128]{3,2,1,0:T(8,128)S(1)} %get-tuple-element.16), channel_id=1, source_target_pairs={{4,0},{8,4},{12,8},{16,12},{20,16},{24,20},{28,24},{32,28},{36,32}... | collective-permute-start | bytes 589832 | tf_op jit(solution)/shard_map/ppermute | solution.py:295
  13.1 0.0 collective-permute-start
  13.8 0.0 copy-done
  13.8 0.0 copy-done.2
  13.8 0.0 copy-done.1
  13.8 0.0 copy-done.3
  13.8 0.0 copy-done.4
  13.8 0.0 copy-done.5
  13.8 4.1 %shard_map.86.part.middle = f32[4,16,16,128]{3,2,1,0:T(8,128)S(1)} custom-call(s32[16]{0:T(128)S(1)} %copy-done.5, s32[1]{0:T(128)S(6)} %copy.9.count, f32[3,4]{1,0:T(4,128)S(1)} %copy-done.4, f32[4,16,16,128]{3,2,1,0:T(8,128)S(1)} %copy-done, f32[16,16,128]{2,1,0:T(8,128)S(1)} %copy-done.1, s32[16,128]{1,0:T(8,128)S(1)} %copy-done.3, ...), custom_call_target="tpu_custom_call" | custom-call | flops 3000000000 | bytes 2097152 | tf_op jit(solution)/shard_map/pallas_call | solution.py:296
  17.9 0.0 collective-permute-done.1.above
  17.9 6.3 %collective-permute-done.below = f32[4,6,16,128]{3,2,1,0:T(8,128)S(1)} collective-permute-done((f32[4,6,16,128]{3,2,1,0:T(8,128)S(1)}, f32[4,6,16,128]{3,2,1,0:T(8,128)S(1)}, u32[]{:S(2)}, u32[]{:S(2)}) %collective-permute-start) | collective-permute-done | bytes 196640 | tf_op jit(solution)/shard_map/ppermute | solution.py:294
  24.3 0.1 shard_map.87
  24.4 1.0 %collective-permute-start.3 = (f32[4,6,16,128]{3,2,1,0:T(8,128)S(1)}, f32[4,6,16,128]{3,2,1,0:T(8,128)S(1)}, u32[]{:S(2)}, u32[]{:S(2)}) collective-permute-start(f32[4,6,16,128]{3,2,1,0:T(8,128)S(1)} %get-tuple-element.9.low), channel_id=1, source_target_pairs={{4,0},{8,4},{12,8},{16,12},{20,16},{24,20},{28,24},{32,28},{36,32}... | collective-permute-start | bytes 589832 | tf_op jit(solution)/shard_map/ppermute | solution.py:302
  25.3 0.6 collective-permute-start.2
  25.9 4.2 %shard_map.88.part = f32[4,16,16,128]{3,2,1,0:T(8,128)S(1)} custom-call(s32[16]{0:T(128)S(1)} %copy-done.5, s32[1]{0:T(128)S(6)} %copy.9.count, f32[3,4]{1,0:T(4,128)S(1)} %copy-done.4, f32[4,16,16,128]{3,2,1,0:T(8,128)S(1)} %copy-done, f32[16,16,128]{2,1,0:T(8,128)S(1)} %copy-done.1, s32[16,128]{1,0:T(8,128)S(1)} %copy-done.3, f32[16,4,128]{2,1,0:T(4,128)S(1)} %copy-done.2, ...), custom_call_target="tpu_custom_call" | custom-call | flops 3000000000 | bytes 2097152 | tf_op jit(solution)/shard_map/pallas_call | solution.py:303
  30.1 0.0 collective-permute-done.3.above
  30.1 5.8 %collective-permute-done.2.below = f32[4,6,16,128]{3,2,1,0:T(8,128)S(1)} collective-permute-done((f32[4,6,16,128]{3,2,1,0:T(8,128)S(1)}, f32[4,6,16,128]{3,2,1,0:T(8,128)S(1)}, u32[]{:S(2)}, u32[]{:S(2)}) %collective-permute-start.2) | collective-permute-done | bytes 196640 | tf_op jit(solution)/shard_map/ppermute | solution.py:301
  35.9 0.9 %shard_map.89 = (f32[4,16,16,128]{3,2,1,0:T(8,128)}, f32[4,4,16,128]{3,2,1,0:T(8,128)S(1)}, f32[4,4,16,128]{3,2,1,0:T(8,128)S(1)}, f32[4,4,16,128]{3,2,1,0:T(8,128)S(1)}, f32[4,4,16,128]{3,2,1,0:T(8,128)S(1)}) custom-call(s32[1]{0:T(128)} %bitcast.me, f32[4,16,16,128]{3,2,1,0:T(8,128)S(1)} %shard_map.88.part, ...), custom_call_target="tpu_custom_call" | custom-call | flops 10000000 | bytes 2097152 | tf_op jit(solution)/shard_map/pallas_call | solution.py:311
  36.9 2.5 %collective-permute-start.4 = (f32[4,4,16,128]{3,2,1,0:T(8,128)S(1)}, f32[4,4,16,128]{3,2,1,0:T(8,128)S(1)}, u32[]{:S(2)}, u32[]{:S(2)}) collective-permute-start(f32[4,4,16,128]{3,2,1,0:T(8,128)S(1)} %get-tuple-element.13), channel_id=1, source_target_pairs={{0,1},{1,0},{2,3},{3,2},{4,5},{5,4},{6,7},{7,6},{8,9},{9,8},{10,11... | collective-permute-start | bytes 393224 | tf_op jit(solution)/shard_map/ppermute | solution.py:316
  39.4 0.4 collective-permute-start.5
  39.8 1.2 %collective-permute-start.6 = (f32[4,4,16,128]{3,2,1,0:T(8,128)S(1)}, f32[4,4,16,128]{3,2,1,0:T(8,128)S(1)}, u32[]{:S(2)}, u32[]{:S(2)}) collective-permute-start(f32[4,4,16,128]{3,2,1,0:T(8,128)S(1)} %get-tuple-element.15), channel_id=1, source_target_pairs={{0,3},{1,2},{2,1},{3,0},{4,7},{5,6},{6,5},{7,4},{8,11},{9,10},{10,... | collective-permute-start | bytes 393224 | tf_op jit(solution)/shard_map/ppermute | solution.py:316
  41.0 0.0 collective-permute-done.4.got_1
  41.0 3.5 %collective-permute-done.5.got_2 = f32[4,4,16,128]{3,2,1,0:T(8,128)S(1)} collective-permute-done((f32[4,4,16,128]{3,2,1,0:T(8,128)S(1)}, f32[4,4,16,128]{3,2,1,0:T(8,128)S(1)}, u32[]{:S(2)}, u32[]{:S(2)}) %collective-permute-start.5) | collective-permute-done | bytes 131104 | tf_op jit(solution)/shard_map/ppermute | solution.py:316
  44.5 2.9 %collective-permute-done.6.got_3 = f32[4,4,16,128]{3,2,1,0:T(8,128)S(1)} collective-permute-done((f32[4,4,16,128]{3,2,1,0:T(8,128)S(1)}, f32[4,4,16,128]{3,2,1,0:T(8,128)S(1)}, u32[]{:S(2)}, u32[]{:S(2)}) %collective-permute-start.6) | collective-permute-done | bytes 131104 | tf_op jit(solution)/shard_map/ppermute | solution.py:316
  47.4 0.8 %shard_map.90 = f32[256,2,128]{2,1,0:T(2,128)S(1)} custom-call(s32[1]{0:T(128)} %bitcast.me, f32[4,4,16,128]{3,2,1,0:T(8,128)S(1)} %get-tuple-element.12.own, f32[4,4,16,128]{3,2,1,0:T(8,128)S(1)} %collective-permute-done.4.got_1, f32[4,4,16,128]{3,2,1,0:T(8,128)S(1)} %collective-permute-done.5.got_2, f32[4,4,16,128]{3,2,1,0:T(8,128)S(1)} %collective-permute-done.6.got_3), custom_call_target="tpu_custom_call" | custom-call | flops 10000000 | bytes 2097152 | tf_op jit(solution)/shard_map/pallas_call | solution.py:320
  48.3 20.8 %all_to_all.5.terms = f32[256,2,128]{2,1,0:T(2,128)S(1)} all-to-all(f32[256,2,128]{2,1,0:T(2,128)S(1)} %shard_map.90), channel_id=1, replica_groups=mesh['dom'=64,'orb'=4] {'dom','orb'}, dimensions={0} | all-to-all | bytes 524288 | tf_op jit(solution)/shard_map/all_to_all | solution.py:326
  69.0 1.0 %shard_map.91 = f32[16,16]{1,0:T(8,128)} custom-call(f32[256,2,128]{2,1,0:T(2,128)S(1)} %all_to_all.5.terms), custom_call_target="tpu_custom_call" | custom-call | flops 10000000 | bytes 2097152 | tf_op jit(solution)/shard_map/pallas_call | solution.py:327
  (2 shorter events, 0.0 us)
Async XLA Ops:
  0.6 13.2 %copy-start = (f32[4,16,16,128]{3,2,1,0:T(8,128)S(1)}, f32[4,16,16,128]{3,2,1,0:T(8,128)}, u32[]{:S(2)}) copy-start(f32[4,16,16,128]{3,2,1,0:T(8,128)} %v.3) | copy-start | bytes 1572868
  0.6 13.2 %copy-start.2 = (f32[16,4,128]{2,1,0:T(4,128)S(1)}, f32[16,4,128]{2,1,0:T(4,128)}, u32[]{:S(2)}) copy-start(f32[16,4,128]{2,1,0:T(4,128)} %projector.3) | copy-start | bytes 98308
  0.6 13.2 %copy-start.1 = (f32[16,16,128]{2,1,0:T(8,128)S(1)}, f32[16,16,128]{2,1,0:T(8,128)}, u32[]{:S(2)}) copy-start(f32[16,16,128]{2,1,0:T(8,128)} %potential.3) | copy-start | bytes 393220
  1.8 12.0 %copy-start.3 = (s32[16,128]{1,0:T(8,128)S(1)}, s32[16,128]{1,0:T(8,128)}, u32[]{:S(2)}) copy-start(s32[16,128]{1,0:T(8,128)} %index.3) | copy-start | bytes 24580
  1.8 16.1 %collective-permute-start.1 = (f32[4,6,16,128]{3,2,1,0:T(8,128)S(1)}, f32[4,6,16,128]{3,2,1,0:T(8,128)S(1)}, u32[]{:S(2)}, u32[]{:S(2)}) collective-permute-start(f32[4,6,16,128]{3,2,1,0:T(8,128)S(1)} %get-tuple-element.16), channel_id=1, source_target_pairs={{4,0},{8,4},{12,8},{16,12},{20,16},{24,20},{28,24},{32,28},{36,32}... | collective-permute-start | bytes 589832 | tf_op jit(solution)/shard_map/ppermute | solution.py:295
  13.1 11.2 %collective-permute-start = (f32[4,6,16,128]{3,2,1,0:T(8,128)S(1)}, f32[4,6,16,128]{3,2,1,0:T(8,128)S(1)}, u32[]{:S(2)}, u32[]{:S(2)}) collective-permute-start(f32[4,6,16,128]{3,2,1,0:T(8,128)S(1)} %get-tuple-element.17), channel_id=1, source_target_pairs={{0,4},{4,8},{8,12},{12,16},{16,20},{20,24},{24,28},{28,32},{32,36}... | collective-permute-start | bytes 589832 | tf_op jit(solution)/shard_map/ppermute | solution.py:294
  13.1 0.7 %copy-start.4 = (f32[3,4]{1,0:T(4,128)S(1)}, f32[3,4]{1,0:T(4,128)}, u32[]{:S(2)}) copy-start(f32[3,4]{1,0:T(4,128)} %energy.3) | copy-start | bytes 148
  13.1 0.7 %copy-start.5 = (s32[16]{0:T(128)S(1)}, s32[16]{0:T(128)}, u32[]{:S(2)}) copy-start(s32[16]{0:T(128)} %species.3) | copy-start | bytes 196
  24.4 5.7 %collective-permute-start.3 = (f32[4,6,16,128]{3,2,1,0:T(8,128)S(1)}, f32[4,6,16,128]{3,2,1,0:T(8,128)S(1)}, u32[]{:S(2)}, u32[]{:S(2)}) collective-permute-start(f32[4,6,16,128]{3,2,1,0:T(8,128)S(1)} %get-tuple-element.9.low), channel_id=1, source_target_pairs={{4,0},{8,4},{12,8},{16,12},{20,16},{24,20},{28,24},{32,28},{36,32}... | collective-permute-start | bytes 589832 | tf_op jit(solution)/shard_map/ppermute | solution.py:302
  25.3 10.6 %collective-permute-start.2 = (f32[4,6,16,128]{3,2,1,0:T(8,128)S(1)}, f32[4,6,16,128]{3,2,1,0:T(8,128)S(1)}, u32[]{:S(2)}, u32[]{:S(2)}) collective-permute-start(f32[4,6,16,128]{3,2,1,0:T(8,128)S(1)} %get-tuple-element.10.high), channel_id=1, source_target_pairs={{0,4},{4,8},{8,12},{12,16},{16,20},{20,24},{24,28},{28,32},{32,36}... | collective-permute-start | bytes 589832 | tf_op jit(solution)/shard_map/ppermute | solution.py:301
  36.9 4.2 %collective-permute-start.4 = (f32[4,4,16,128]{3,2,1,0:T(8,128)S(1)}, f32[4,4,16,128]{3,2,1,0:T(8,128)S(1)}, u32[]{:S(2)}, u32[]{:S(2)}) collective-permute-start(f32[4,4,16,128]{3,2,1,0:T(8,128)S(1)} %get-tuple-element.13), channel_id=1, source_target_pairs={{0,1},{1,0},{2,3},{3,2},{4,5},{5,4},{6,7},{7,6},{8,9},{9,8},{10,11... | collective-permute-start | bytes 393224 | tf_op jit(solution)/shard_map/ppermute | solution.py:316
  39.4 5.1 %collective-permute-start.5 = (f32[4,4,16,128]{3,2,1,0:T(8,128)S(1)}, f32[4,4,16,128]{3,2,1,0:T(8,128)S(1)}, u32[]{:S(2)}, u32[]{:S(2)}) collective-permute-start(f32[4,4,16,128]{3,2,1,0:T(8,128)S(1)} %get-tuple-element.14), channel_id=1, source_target_pairs={{0,2},{1,3},{2,0},{3,1},{4,6},{5,7},{6,4},{7,5},{8,10},{9,11},{10,... | collective-permute-start | bytes 393224 | tf_op jit(solution)/shard_map/ppermute | solution.py:316
  39.8 7.6 %collective-permute-start.6 = (f32[4,4,16,128]{3,2,1,0:T(8,128)S(1)}, f32[4,4,16,128]{3,2,1,0:T(8,128)S(1)}, u32[]{:S(2)}, u32[]{:S(2)}) collective-permute-start(f32[4,4,16,128]{3,2,1,0:T(8,128)S(1)} %get-tuple-element.15), channel_id=1, source_target_pairs={{0,3},{1,2},{2,1},{3,0},{4,7},{5,6},{6,5},{7,4},{8,11},{9,10},{10,... | collective-permute-start | bytes 393224 | tf_op jit(solution)/shard_map/ppermute | solution.py:316

commit v2 on v1

v2 whole, which is shorter than its diff:
```python
import functools

import jax
import jax.numpy as jnp
from jax import lax
from jax.experimental import pallas as pl
from jax.experimental.pallas import tpu as pltpu
from jax.sharding import PartitionSpec as P

RADIUS = 6
STENCIL = (
    -5369.0 / 1800.0,
    12.0 / 7.0,
    -15.0 / 56.0,
    10.0 / 189.0,
    -1.0 / 112.0,
    2.0 / 1925.0,
    -1.0 / 16632.0,
)
LOWER_EDGE = 2.0
UPPER_EDGE = 17.0
MID_POINT = 0.5 * (UPPER_EDGE + LOWER_EDGE)
HALF_WIDTH = 0.5 * (UPPER_EDGE - LOWER_EDGE)
VMEM = pltpu.VMEM
NT = (((1,), (1,)), ((), ()))


def split(values):
    high = values.astype(jnp.bfloat16)
    return high, (values - high.astype(jnp.float32)).astype(jnp.bfloat16)


def place(condition):
    return jnp.where(condition, 1.0, 0.0).astype(jnp.bfloat16)


def mark_cells(index, rowhot, zhot):
    cells = index[...]
    row_of = cells >> 7
    lane_of = cells & 127
    row_iota = lax.broadcasted_iota(jnp.int32, (256, 128), 0)
    for a in range(cells.shape[0]):
        at = slice(a * 128, (a + 1) * 128)
        rowhot[:, at] = place(row_iota == row_of[a : a + 1])
        zhot[:, at] = place(row_iota[:128] == lane_of[a : a + 1])


def nonlocal_rows(load_rows, orbs, index, projector, strength, parts, rowhot, zhot, picked, spread):
    lanes = 128
    atoms, channels = projector.shape[0], projector.shape[1]
    for o in range(orbs):
        high, low = split(load_rows(o).T)
        parts[0, o * lanes : (o + 1) * lanes, :] = high
        parts[1, o * lanes : (o + 1) * lanes, :] = low
    cells = index[...]
    lane_of = cells & 127
    lane_iota = lax.broadcasted_iota(jnp.int32, (lanes, lanes), 0)
    for a in range(0, atoms, 2):
        at = slice(a * lanes, (a + 2) * lanes)
        found = jnp.dot(parts[0], rowhot[:, at], preferred_element_type=jnp.float32)
        found = found + jnp.dot(parts[1], rowhot[:, at], preferred_element_type=jnp.float32)
        for b in range(2):
            hot = lane_iota == lane_of[a + b : a + b + 1]
            for o in range(orbs):
                block = found[o * lanes : (o + 1) * lanes, b * lanes : (b + 1) * lanes]
                picked[o, a + b : a + b + 1, :] = jnp.sum(
                    jnp.where(hot, block, 0.0), axis=0, keepdims=True
                )
    inside = cells >= 0
    total = [jnp.zeros((atoms, lanes), jnp.float32) for _ in range(orbs)]
    for p in range(channels):
        shape = projector[:, p, :]
        for o in range(orbs):
            coefficient = jnp.sum(shape * picked[o], axis=1, keepdims=True)
            total[o] = total[o] + shape * (coefficient * strength[p])
    for o in range(orbs):
        high, low = split(jnp.where(inside, total[o], 0.0))
        for a in range(atoms):
            at = slice(a * lanes, (a + 1) * lanes)
            hot = zhot[:, at]
            spread[0, o * lanes : (o + 1) * lanes, at] = hot * high[a : a + 1]
            spread[1, o * lanes : (o + 1) * lanes, at] = hot * low[a : a + 1]
    out = lax.dot_general(rowhot[...], spread[0], NT, preferred_element_type=jnp.float32)
    return out + lax.dot_general(rowhot[...], spread[1], NT, preferred_element_type=jnp.float32)


def local_layer(load, potential, i, layers):
    centre = load(i)
    total = (potential - (1.5 * STENCIL[0] + MID_POINT)) * centre
    for k in range(1, RADIUS + 1):
        near = pltpu.roll(centre, k, 0) + pltpu.roll(centre, centre.shape[0] - k, 0)
        near = near + pltpu.roll(centre, k, 1) + pltpu.roll(centre, centre.shape[1] - k, 1)
        if i - k >= 0:
            near = near + load(i - k)
        if i + k < layers:
            near = near + load(i + k)
        total = total - (0.5 * STENCIL[k]) * near
    return total


def first_kernel(
    species,
    count,
    energy,
    v,
    potential,
    index,
    projector,
    out,
    rowhot,
    zhot,
    strength,
    parts,
    picked,
    spread,
):
    orbs, layers = v.shape[0], v.shape[1]
    slot_strengths(species, count, energy, strength)
    mark_cells(index, rowhot, zhot)
    hat = nonlocal_rows(
        lambda o: v[o].reshape(256, 128),
        orbs,
        index,
        projector,
        strength,
        parts,
        rowhot,
        zhot,
        picked,
        spread,
    )
    for o in range(orbs):
        for i in range(layers):
            total = local_layer(lambda j: v[o, j], potential[i], i, layers)
            total = total + hat[i * 16 : (i + 1) * 16, o * 128 : (o + 1) * 128]
            out[o, i] = total * (1.0 / HALF_WIDTH)


def second_kernel(
    v,
    potential,
    index,
    projector,
    strength,
    rowhot,
    zhot,
    near,
    far,
    middle,
    out,
    parts,
    picked,
    spread,
    held,
):
    orbs, layers = v.shape[0], v.shape[1]
    first, last = far_near_starts(layers)
    held[:, pl.ds(first, RADIUS)] = far[...]
    held[:, pl.ds(last, RADIUS)] = near[...]
    held[:, RADIUS : layers - RADIUS] = middle[:, RADIUS : layers - RADIUS]
    hat = nonlocal_rows(
        lambda o: held[o].reshape(256, 128),
        orbs,
        index,
        projector,
        strength,
        parts,
        rowhot,
        zhot,
        picked,
        spread,
    )
    for o in range(orbs):
        for i in range(layers):
            total = local_layer(lambda j: held[o, j], potential[i], i, layers)
            total = total + hat[i * 16 : (i + 1) * 16, o * 128 : (o + 1) * 128]
            out[o, i] = total * (2.0 / HALF_WIDTH) - v[o, i]


def from_below(below, o, i):
    total = STENCIL[i + 1] * below[o, RADIUS - 1]
    for k in range(i + 2, RADIUS + 1):
        total = total + STENCIL[k] * below[o, RADIUS + i - k]
    return total


def from_above(above, o, j):
    total = STENCIL[j + 1] * above[o, 0]
    for k in range(j + 2, RADIUS + 1):
        total = total + STENCIL[k] * above[o, k - j - 1]
    return total


def far_near_starts(layers):
    odd = lax.axis_index("dom") & 1
    first = odd * (layers - RADIUS)
    return first, layers - RADIUS - first


def by_parity(body, far, near):
    odd = lax.axis_index("dom") & 1

    @pl.when(odd == 0)
    def _():
        body(far, near)

    @pl.when(odd == 1)
    def _():
        body(near, far)


def order_edges(low, high, far, near):
    def body(far_edge, near_edge):
        far[...] = far_edge[...]
        near[...] = near_edge[...]

    by_parity(body, low, high)


def slot_strengths(species, count, energy, strength):
    channels, atoms = strength.shape[0], strength.shape[1]
    slot = lax.broadcasted_iota(jnp.int32, (atoms, 128), 0)
    live = slot < count[0]
    for p in range(channels):
        total = jnp.zeros((atoms, 128), jnp.float32)
        for a in range(atoms):
            total = jnp.where(slot == a, energy[species[a], p], total)
        strength[p] = jnp.where(live, total, 0.0)


def first_edge(far_side, part, got, edge):
    orbs, layers = part.shape[0], part.shape[1]
    scale = -0.5 / HALF_WIDTH
    odd = lax.axis_index("dom") & 1

    @pl.when(odd == (0 if far_side else 1))
    def _():
        for o in range(orbs):
            for i in range(RADIUS):
                edge[o, i] = part[o, i] + scale * from_below(got, o, i)

    @pl.when(odd == (1 if far_side else 0))
    def _():
        for o in range(orbs):
            for i in range(RADIUS):
                at = layers - 1 - i
                edge[o, RADIUS - 1 - i] = part[o, at] + scale * from_above(got, o, i)


def deal(block, chunks):
    me = lax.axis_index("orb")
    depth = chunks[0].shape[1]
    for k, chunk in enumerate(chunks):
        first = (me ^ k) * depth
        for o in range(block.shape[0]):
            chunk[o] = block[o, pl.ds(first, depth)]


def second_near(part, got, block, *chunks):
    orbs, layers = part.shape[0], part.shape[1]
    scale = -1.0 / HALF_WIDTH
    odd = lax.axis_index("dom") & 1

    @pl.when(odd == 0)
    def _():
        for o in range(orbs):
            for i in range(RADIUS, layers):
                rows = part[o, i]
                if i >= layers - RADIUS:
                    rows = rows + scale * from_above(got, o, layers - 1 - i)
                block[o, 2 * (i - RADIUS) : 2 * (i - RADIUS) + 2] = rows.reshape(2, 8, 128)

    @pl.when(odd == 1)
    def _():
        for o in range(orbs):
            for i in range(layers - RADIUS):
                rows = part[o, i]
                if i < RADIUS:
                    rows = rows + scale * from_below(got, o, i)
                block[o, 2 * i : 2 * i + 2] = rows.reshape(2, 8, 128)

    deal(block, chunks)


def second_far(part, got, block, *chunks):
    orbs, layers = part.shape[0], part.shape[1]
    scale = -1.0 / HALF_WIDTH
    odd = lax.axis_index("dom") & 1

    @pl.when(odd == 0)
    def _():
        for o in range(orbs):
            for i in range(RADIUS):
                rows = part[o, i] + scale * from_below(got, o, i)
                block[o, 2 * i : 2 * i + 2] = rows.reshape(2, 8, 128)

    @pl.when(odd == 1)
    def _():
        for o in range(orbs):
            for i in range(RADIUS):
                rows = part[o, layers - 1 - i] + scale * from_above(got, o, i)
                at = 2 * (RADIUS - 1 - i)
                block[o, at : at + 2] = rows.reshape(2, 8, 128)

    deal(block, chunks)


def split_3(values):
    high = values.astype(jnp.bfloat16)
    rest = values - high.astype(jnp.float32)
    middle = rest.astype(jnp.bfloat16)
    low = (rest - middle.astype(jnp.float32)).astype(jnp.bfloat16)
    return jnp.concatenate([high, middle, low], axis=0)


def lane_block(lane):
    block = lane >> 4
    first = jnp.where(block < 3, 0, jnp.where(block < 5, 1, 2))
    second = jnp.where(block < 3, block + 1, jnp.where(block < 5, block - 1, 3))
    return block, 4 * first + ((lane >> 2) & 3), 4 * second + (lane & 3)


def row_products(loads, rows, left_rows, right_rows):
    total = None
    for load in loads:
        high, low = split(load().reshape(rows, 128))
        left = jnp.concatenate([high, high, low], axis=1)[left_rows]
        right = jnp.concatenate([high, low, high], axis=1)[right_rows]
        term = lax.dot_general(left, right, NT, preferred_element_type=jnp.float32)
        total = term if total is None else total + term
    row = lax.broadcasted_iota(jnp.int32, total.shape, 0)
    column = lax.broadcasted_iota(jnp.int32, total.shape, 1)
    total = jnp.where((row & 7) == (column & 7), total, 0.0)
    return jnp.sum(total.reshape(total.shape[0] // 8, 8, total.shape[1]), axis=1)


def pack(sums, column_orbital, row_orbital):
    count, columns = sums.shape
    lane = lax.broadcasted_iota(jnp.int32, (columns, 128), 1)
    orbital = lax.broadcasted_iota(jnp.int32, (columns, 128), 0) >> 3
    wide = jnp.dot(
        split_3(sums),
        place(orbital == column_orbital(lane)),
        preferred_element_type=jnp.float32,
    )
    wide = wide[:count] + wide[count : 2 * count] + wide[2 * count :]
    lane = lax.broadcasted_iota(jnp.int32, (count, 128), 1)
    orbital = lax.broadcasted_iota(jnp.int32, (count, 128), 0)
    return jnp.sum(jnp.where(orbital == row_orbital(lane), wide, 0.0), axis=0, keepdims=True)


def own_gram(early, near, far, out, own):
    orbs, layers = out.shape[0], out.shape[1]
    first, _ = far_near_starts(layers)
    rest = RADIUS - (first * RADIUS) // (layers - RADIUS)
    out[:, pl.ds(first, RADIUS)] = far[...].reshape(orbs, RADIUS, 16, 128)
    out[:, pl.ds(rest, layers - RADIUS)] = near[...].reshape(orbs, layers - RADIUS, 16, 128)
    everything = slice(None)
    loads = [lambda h=h: near[:, h] for h in range(near.shape[1])]
    loads += [lambda h=h: far[:, h] for h in range(far.shape[1])]
    sums = row_products(loads, 8 * orbs, everything, everything)
    sums = jnp.concatenate([sums, jnp.zeros_like(sums)], axis=0)
    lanes = pack(sums, lambda lane: lane & 3, lambda lane: (lane >> 2) & 3)
    lane = lax.broadcasted_iota(jnp.int32, (1, 128), 1)
    own[...] = early[...] + jnp.where((lane >= 96) & (lane < 112), lanes, 0.0)


def gram_lanes(chunks, rows):
    orbs, depth = chunks[0].shape[0], chunks[0].shape[1]
    me = lax.axis_index("orb")
    for k, chunk in enumerate(chunks):
        first = (me ^ k) * orbs
        for o in range(orbs):
            for h in range(depth):
                rows[h, first + o] = chunk[o, h]
    loads = [lambda h=h: rows[h] for h in range(depth)]
    sums = row_products(loads, 128, slice(0, 96), slice(32, 128))
    sums = jnp.concatenate([sums, jnp.zeros((4, 96), jnp.float32)], axis=0)
    lanes = pack(sums, lambda lane: lane_block(lane)[2] - 4, lambda lane: lane_block(lane)[1])
    lane = lax.broadcasted_iota(jnp.int32, (1, 128), 1)
    return jnp.where(lane < 96, lanes, 0.0)


def near_gram(got_2, got_3, got_1, own, out, rows):
    out[...] = gram_lanes((own, got_1, got_2, got_3), rows)


def far_gram(others, got_2, got_3, got_1, own, out, rows):
    lanes = gram_lanes((own, got_1, got_2, got_3), rows) + others[...]
    out[...] = jnp.broadcast_to(lanes[None], out.shape)


def final_kernel(cells, terms, out):
    orbs = 4
    sums = [terms[q] for q in range(orbs)]
    for d in range(1, terms.shape[0] // orbs):
        for q in range(orbs):
            sums[q] = sums[q] + terms[d * orbs + q]
    across = sums[0] + sums[1] + sums[2] + sums[3]
    row = lax.broadcasted_iota(jnp.int32, (16, 128), 0)
    lane = lax.broadcasted_iota(jnp.int32, (16, 128), 1)
    block, first, second = lane_block(lane)
    own = jnp.where(
        row < 8,
        jnp.where(row < 4, sums[0], sums[1]),
        jnp.where(row < 12, sums[2], sums[3]),
    )
    upper = jnp.where((block < 6) & (first == row), across, 0.0)
    lower = jnp.where((block < 6) & (second == row), across, 0.0)
    own = jnp.where((block == 6) & (((lane >> 2) & 3) == (row & 3)), own, 0.0)
    column = lax.broadcasted_iota(jnp.int32, (128, 16), 1)
    lane = lax.broadcasted_iota(jnp.int32, (128, 16), 0)
    block, first, second = lane_block(lane)

    def unpack(values, condition):
        parts = jnp.dot(split_3(values), place(condition), preferred_element_type=jnp.float32)
        return parts[:16] + parts[16:32] + parts[32:]

    total = unpack(upper, second == column) + unpack(lower, first == column)
    same = (lax.broadcasted_iota(jnp.int32, (16, 16), 0) >> 2) == (
        lax.broadcasted_iota(jnp.int32, (16, 16), 1) >> 2
    )
    total = total + jnp.where(same, unpack(own, (lane & 3) == (column & 3)), 0.0)
    out[...] = total * (1.0 / cells)


def call(kernel, outs, in_specs, scratch=(), flops=10_000_000, limit=48 * 2**20):
    return pl.pallas_call(
        kernel,
        out_shape=outs,
        in_specs=in_specs,
        out_specs=jax.tree.map(lambda _: pl.BlockSpec(memory_space=VMEM), outs),
        scratch_shapes=list(scratch),
        compiler_params=pltpu.CompilerParams(vmem_limit_bytes=limit),
        cost_estimate=pl.CostEstimate(flops=flops, bytes_accessed=2**21, transcendentals=0),
    )


def on_device(
    orbitals, local_potential, sphere_index, projector, species, atom_count, channel_energy
):
    f32 = jnp.float32
    in_vmem = pl.BlockSpec(memory_space=VMEM)
    orbs, layers, wide, deep = orbitals.shape
    doms, orb_devices = lax.axis_size("dom"), lax.axis_size("orb")
    far_pairs = [(i, (i - 1 if i % 2 == 0 else i + 1) % doms) for i in range(doms)]
    near_pairs = [(i, i ^ 1) for i in range(doms)]
    edge = jax.ShapeDtypeStruct((orbs, RADIUS, wide, deep), f32)
    block = jax.ShapeDtypeStruct(orbitals.shape, f32)
    atoms, points = sphere_index.shape
    in_smem = pl.BlockSpec(memory_space=pltpu.SMEM)
    scalars = (species, atom_count, channel_energy)
    fields = (orbitals, local_potential, sphere_index, projector)
    far, near = call(order_edges, (edge, edge), [in_vmem] * 2)(
        orbitals[:, :RADIUS], orbitals[:, layers - RADIUS :]
    )
    got_far = lax.ppermute(far, "dom", far_pairs)
    got_near = lax.ppermute(near, "dom", near_pairs)
    scratch = [
        pltpu.VMEM((2, orbs * deep, layers * wide), jnp.bfloat16),
        pltpu.VMEM((orbs,) + sphere_index.shape, f32),
        pltpu.VMEM((2, orbs * deep, atoms * points), jnp.bfloat16),
    ]
    part, rowhot, zhot, strength = call(
        first_kernel,
        (
            block,
            jax.ShapeDtypeStruct((layers * wide, atoms * points), jnp.bfloat16),
            jax.ShapeDtypeStruct((deep, atoms * points), jnp.bfloat16),
            jax.ShapeDtypeStruct((projector.shape[1], atoms, deep), f32),
        ),
        [in_smem] * 3 + [in_vmem] * 4,
        scratch,
        flops=3_000_000_000,
    )(*scalars, *fields)
    near = call(functools.partial(first_edge, False), edge, [in_vmem] * 2)(part, got_near)
    got_near = lax.ppermute(near, "dom", near_pairs)
    far = call(functools.partial(first_edge, True), edge, [in_vmem] * 2)(part, got_far)
    got_far = lax.ppermute(far, "dom", far_pairs)
    part = call(
        second_kernel,
        block,
        [in_vmem] * 10,
        scratch + [pltpu.VMEM(orbitals.shape, f32)],
        flops=3_000_000_000,
    )(*fields, strength, rowhot, zhot, near, far, part)

    def halves(count):
        return jax.ShapeDtypeStruct((orbs, 2 * count, wide // 2, deep), f32)

    def swap(chunks):
        return {
            k: lax.ppermute(chunks[k], "orb", [(i, i ^ k) for i in range(orb_devices)])
            for k in (2, 3, 1)
        }

    def rows_of(chunk):
        return [pltpu.VMEM((chunk.shape[1], orbs * orb_devices) + chunk.shape[2:], f32)]

    def chunk(count):
        return jax.ShapeDtypeStruct((orbs, 2 * count // orb_devices, wide // 2, deep), f32)

    row = jax.ShapeDtypeStruct((1, 128), f32)
    inner = layers - RADIUS
    near, *sends = call(second_near, (halves(inner),) + (chunk(inner),) * 4, [in_vmem] * 2)(
        part, got_near
    )
    own_near, got_early = sends[0], swap(sends)
    far, *sends = call(second_far, (halves(RADIUS),) + (chunk(RADIUS),) * 4, [in_vmem] * 2)(
        part, got_far
    )
    own_far, got_late = sends[0], swap(sends)
    early = call(near_gram, row, [in_vmem] * 4, rows_of(own_near), flops=1_000_000_000)(
        got_early[2], got_early[3], got_early[1], own_near
    )
    filtered, others = call(own_gram, (block, row), [in_vmem] * 3, flops=1_500_000_000)(
        early, near, far
    )
    terms = call(
        far_gram,
        jax.ShapeDtypeStruct((doms * orb_devices, 1, 128), f32),
        [in_vmem] * 5,
        rows_of(own_far),
    )(others, got_late[2], got_late[3], got_late[1], own_far)
    terms = lax.all_to_all(terms, ("dom", "orb"), 0, 0)
    gram = call(
        functools.partial(final_kernel, float(layers * wide * deep * doms)),
        jax.ShapeDtypeStruct((16, 16), f32),
        [in_vmem],
    )(terms)
    return filtered, gram


def solution(mesh):
    placed = (
        P("orb", "dom", None, None),
        P("dom", None, None),
        P("dom", None),
        P("dom", None, None),
        P("dom"),
        P("dom"),
        P(),
    )
    return jax.shard_map(
        on_device,
        mesh=mesh,
        in_specs=placed,
        out_specs=(P("orb", "dom", None, None), P()),
        check_vma=False,
    )
```

time: 70.2 us -> 60.1 us (0.86)
  waiting for transfers between devices: 18.5 us -> 1.38 us
  starting transfers between devices: 17 us -> 25.1 us
  blocking collectives: 20.8 us -> 19.4 us
    ppermute x7 -> x10, waiting for transfers between devices: 18.5 us -> 1.38 us  [the longest x6 1.37 us: swap(): lax.ppermute(chunks[k], 'orb', [(i, i ^ k) for i in range(orb_devices)])]
    ppermute x7 -> x10, starting transfers between devices: 17 us -> 25.1 us  [the longest x2 15.6 us: on_device(): got_far = lax.ppermute(far, 'dom', far_pairs)]
    all_to_all x1, blocking collectives: 20.8 us -> 19.4 us  [on_device(): terms = lax.all_to_all(terms, ('dom', 'orb'), 0, 0)]
    pallas_call x5 -> x10, Pallas kernels: 10.1 us -> 10.6 us  [the longest x1 4.47 us: on_device(): call(first_kernel, (block, jax.ShapeDtypeStruct((layers * wide, atoms * p...]
  transfers between devices with their start and end apart: 7 -> 10, of which waited for: 4 -> 1; matrix products, arithmetic and copies ran while one was open for 0% -> 0% of each run, Pallas kernels for 12% -> 17%
where the time goes in v2:
time: 60.1 us; the launch traced here: 60 us
  starting transfers between devices  25.1 us (42%)
  blocking collectives  19.4 us (32%)
  Pallas kernels  11.4 us (19%)
  between operations  1.48 us (2%)
  waiting for transfers between devices  1.38 us (2%)
  local copies, waits for them, and re-layouts  1.14 us (2%)
    all_to_all x1, blocking collectives, on_device(): terms = lax.all_to_all(terms, ('dom', 'orb'), 0, 0)  19.4 us
    ppermute x2, starting transfers between devices, on_device(): got_far = lax.ppermute(far, 'dom', far_pairs)  15.6 us
    ppermute x6, starting transfers between devices, swap(): lax.ppermute(chunks[k], 'orb', [(i, i ^ k) for i in range(orb_devices)])  7.33 us
    pallas_call x1, Pallas kernels, on_device(): call(first_kernel, (block, jax.ShapeDtypeStruct((layers * wide, atoms * p...  4.47 us
    pallas_call x1, Pallas kernels, on_device(): call(second_kernel, block, [in_vmem] * 10, scratch + [pltpu.VMEM(orbitals...  3.51 us
    ppermute x2, starting transfers between devices, on_device(): got_near = lax.ppermute(near, 'dom', near_pairs)  2.22 us
    ppermute x6, waiting for transfers between devices, swap(): lax.ppermute(chunks[k], 'orb', [(i, i ^ k) for i in range(orb_devices)])  1.37 us
    pallas_call x1, Pallas kernels, on_device(): call(own_gram, (block, row), [in_vmem] * 3, flops=1500000000)  1.24 us
  transfers between devices with their start and end apart: 10, of which 1 were waited for; matrix products, arithmetic and copies ran while one was open for 0% of the time, Pallas kernels for 17%

profile of v2, /device:TPU:1, one launch (start us, length us, event | category | flops | bytes accessed | tf_op | source)
XLA Modules:
  0.0 60.0 jit_solution(327549242903100987)
XLA Ops:
  0.6 1.1 %fusion = (f32[4,6,16,128]{3,2,1,0:T(8,128)S(1)}, f32[4,6,16,128]{3,2,1,0:T(8,128)S(1)}) fusion(f32[4,16,16,128]{3,2,1,0:T(8,128)} %v.3), kind=kLoop, calls=%fused_computation | loop fusion | bytes 786432 | tf_op jit(solution)/shard_map/slice | solution.py:455
  1.8 0.0 copy-start.1
  1.8 0.0 copy-start.2
  1.8 0.0 copy-start.3
  1.8 0.0 copy-start.4
  1.9 2.1 %collective-permute-start = (f32[4,6,16,128]{3,2,1,0:T(8,128)S(1)}, f32[4,6,16,128]{3,2,1,0:T(8,128)S(1)}, u32[]{:S(2)}, u32[]{:S(2)}) collective-permute-start(f32[4,6,16,128]{3,2,1,0:T(8,128)S(1)} %get-tuple-element.24), channel_id=1, source_target_pairs={{0,4},{4,0},{8,12},{12,8},{16,20},{20,16},{24,28},{28,24},{32,36},... | collective-permute-start | bytes 589832 | tf_op jit(solution)/shard_map/ppermute | solution.py:458
  4.0 9.7 %collective-permute-start.1 = (f32[4,6,16,128]{3,2,1,0:T(8,128)S(1)}, f32[4,6,16,128]{3,2,1,0:T(8,128)S(1)}, u32[]{:S(2)}, u32[]{:S(2)}) collective-permute-start(f32[4,6,16,128]{3,2,1,0:T(8,128)S(1)} %get-tuple-element.25), channel_id=1, source_target_pairs={{0,252},{4,8},{8,4},{12,16},{16,12},{20,24},{24,20},{28,32},{32,28... | collective-permute-start | bytes 589832 | tf_op jit(solution)/shard_map/ppermute | solution.py:457
  14.4 4.5 %shard_map.86 = (f32[4,16,16,128]{3,2,1,0:T(8,128)S(1)}, bf16[256,2048]{1,0:T(8,128)(2,1)S(1)}, bf16[128,2048]{1,0:T(8,128)(2,1)S(1)}, f32[4,16,128]{2,1,0:T(8,128)S(1)}) custom-call(s32[16]{0:T(128)S(1)} %copy-done.5, s32[1]{0:T(128)S(6)} %copy.9.count, f32[3,4]{1,0:T(4,128)S(1)} %copy-done.4, f32[4,16,16,128]{3,2,1,0:T(8,128)S(1)} %copy-done, ...), custom_call_target="tpu_custom_call" | custom-call | flops 3000000000 | bytes 2097152 | tf_op jit(solution)/shard_map/pallas_call | solution.py:464
  18.9 0.0 collective-permute-done.got
  18.9 0.1 shard_map.88.near
  19.0 0.1 collective-permute-start.2
  19.1 0.0 collective-permute-done.1.got
  19.1 0.1 shard_map.89.far
  19.2 5.8 %collective-permute-start.6 = (f32[4,6,16,128]{3,2,1,0:T(8,128)S(1)}, f32[4,6,16,128]{3,2,1,0:T(8,128)S(1)}, u32[]{:S(2)}, u32[]{:S(2)}) collective-permute-start(f32[4,6,16,128]{3,2,1,0:T(8,128)S(1)} %shard_map.89.far), channel_id=1, source_target_pairs={{0,252},{4,8},{8,4},{12,16},{16,12},{20,24},{24,20},{28,32},{32,28... | collective-permute-start | bytes 589832 | tf_op jit(solution)/shard_map/ppermute | solution.py:479
  25.0 3.5 %shard_map.90.part = f32[4,16,16,128]{3,2,1,0:T(8,128)S(1)} custom-call(f32[4,16,16,128]{3,2,1,0:T(8,128)S(1)} %copy-done, f32[16,16,128]{2,1,0:T(8,128)S(1)} %copy-done.1, s32[16,128]{1,0:T(8,128)S(1)} %copy-done.3, f32[16,4,128]{2,1,0:T(4,128)S(1)} %copy-done.2, f32[4,16,128]{2,1,0:T(8,128)S(1)} %get-tuple-element.20.strength, ...), custom_call_target="tpu_custom_call" | custom-call | flops 3000000000 | bytes 2097152 | tf_op jit(solution)/shard_map/pallas_call | solution.py:480
  28.6 0.0 collective-permute-done.2.got
  28.6 0.1 shard_map.91
  28.7 0.5 collective-permute-start.3
  29.2 3.4 %collective-permute-start.4 = (f32[4,5,8,128]{3,2,1,0:T(8,128)S(1)}, f32[4,5,8,128]{3,2,1,0:T(8,128)S(1)}, u32[]{:S(2)}, u32[]{:S(2)}) collective-permute-start(f32[4,5,8,128]{3,2,1,0:T(8,128)S(1)} %get-tuple-element.27), channel_id=1, source_target_pairs={{0,3},{1,2},{2,1},{3,0},{4,7},{5,6},{6,5},{7,4},{8,11},{9,10},{10,... | collective-permute-start | bytes 245768 | tf_op jit(solution)/shard_map/ppermute | solution.py:493
  32.5 0.0 collective-permute-start.5
  32.5 0.0 collective-permute-done.6.got
  32.5 0.1 shard_map.93
  32.6 0.7 %collective-permute-start.7 = (f32[4,3,8,128]{3,2,1,0:T(8,128)S(1)}, f32[4,3,8,128]{3,2,1,0:T(8,128)S(1)}, u32[]{:S(2)}, u32[]{:S(2)}) collective-permute-start(f32[4,3,8,128]{3,2,1,0:T(8,128)S(1)} %get-tuple-element.34), channel_id=1, source_target_pairs={{0,2},{1,3},{2,0},{3,1},{4,6},{5,7},{6,4},{7,5},{8,10},{9,11},{10,... | collective-permute-start | bytes 147464 | tf_op jit(solution)/shard_map/ppermute | solution.py:493
  33.3 1.7 %collective-permute-start.8 = (f32[4,3,8,128]{3,2,1,0:T(8,128)S(1)}, f32[4,3,8,128]{3,2,1,0:T(8,128)S(1)}, u32[]{:S(2)}, u32[]{:S(2)}) collective-permute-start(f32[4,3,8,128]{3,2,1,0:T(8,128)S(1)} %get-tuple-element.35), channel_id=1, source_target_pairs={{0,3},{1,2},{2,1},{3,0},{4,7},{5,6},{6,5},{7,4},{8,11},{9,10},{10,... | collective-permute-start | bytes 147464 | tf_op jit(solution)/shard_map/ppermute | solution.py:493
  35.0 1.1 %collective-permute-start.9 = (f32[4,3,8,128]{3,2,1,0:T(8,128)S(1)}, f32[4,3,8,128]{3,2,1,0:T(8,128)S(1)}, u32[]{:S(2)}, u32[]{:S(2)}) collective-permute-start(f32[4,3,8,128]{3,2,1,0:T(8,128)S(1)} %get-tuple-element.36), channel_id=1, source_target_pairs={{0,1},{1,0},{2,3},{3,2},{4,5},{5,4},{6,7},{7,6},{8,9},{9,8},{10,11... | collective-permute-start | bytes 147464 | tf_op jit(solution)/shard_map/ppermute | solution.py:493
  36.1 1.4 %collective-permute-done.4.got_3 = f32[4,5,8,128]{3,2,1,0:T(8,128)S(1)} collective-permute-done((f32[4,5,8,128]{3,2,1,0:T(8,128)S(1)}, f32[4,5,8,128]{3,2,1,0:T(8,128)S(1)}, u32[]{:S(2)}, u32[]{:S(2)}) %collective-permute-start.4) | collective-permute-done | bytes 81952 | tf_op jit(solution)/shard_map/ppermute | solution.py:493
  37.5 0.0 collective-permute-done.5.got_1
  37.5 0.5 shard_map.92.early
  38.0 1.2 %shard_map.94 = (f32[4,16,16,128]{3,2,1,0:T(8,128)}, f32[1,128]{1,0:T(1,128)S(1)}) custom-call(f32[1,128]{1,0:T(1,128)S(1)} %shard_map.92.early, f32[4,20,8,128]{3,2,1,0:T(8,128)S(1)} %get-tuple-element.30.near, f32[4,12,8,128]{3,2,1,0:T(8,128)S(1)} %get-tuple-element.31.far), custom_call_target="tpu_custom_call" | custom-call | flops 1500000000 | bytes 2097152 | tf_op jit(solution)/shard_map/pallas_call | solution.py:516
  39.2 0.5 shard_map.95
  39.7 19.4 %all_to_all.5.terms = f32[256,1,128]{2,1,0:T(1,128)S(1)} all-to-all(f32[256,1,128]{2,1,0:T(1,128)S(1)} %shard_map.95), channel_id=1, replica_groups=mesh['dom'=64,'orb'=4] {'dom','orb'}, dimensions={0} | all-to-all | bytes 262144 | tf_op jit(solution)/shard_map/all_to_all | solution.py:525
  59.1 0.9 %shard_map.96 = f32[16,16]{1,0:T(8,128)} custom-call(f32[256,1,128]{2,1,0:T(1,128)S(1)} %all_to_all.5.terms), custom_call_target="tpu_custom_call" | custom-call | flops 10000000 | bytes 2097152 | tf_op jit(solution)/shard_map/pallas_call | solution.py:526
  (13 shorter events, 0.1 us)
Async XLA Ops:
  0.6 13.7 %copy-start = (f32[4,16,16,128]{3,2,1,0:T(8,128)S(1)}, f32[4,16,16,128]{3,2,1,0:T(8,128)}, u32[]{:S(2)}) copy-start(f32[4,16,16,128]{3,2,1,0:T(8,128)} %v.3) | copy-start | bytes 1572868
  1.8 12.6 %copy-start.1 = (f32[16,16,128]{2,1,0:T(8,128)S(1)}, f32[16,16,128]{2,1,0:T(8,128)}, u32[]{:S(2)}) copy-start(f32[16,16,128]{2,1,0:T(8,128)} %potential.3) | copy-start | bytes 393220
  1.8 12.6 %copy-start.2 = (f32[16,4,128]{2,1,0:T(4,128)S(1)}, f32[16,4,128]{2,1,0:T(4,128)}, u32[]{:S(2)}) copy-start(f32[16,4,128]{2,1,0:T(4,128)} %projector.3) | copy-start | bytes 98308
  1.8 12.6 %copy-start.3 = (s32[16,128]{1,0:T(8,128)S(1)}, s32[16,128]{1,0:T(8,128)}, u32[]{:S(2)}) copy-start(s32[16,128]{1,0:T(8,128)} %index.3) | copy-start | bytes 24580
  1.8 12.6 %copy-start.4 = (f32[3,4]{1,0:T(4,128)S(1)}, f32[3,4]{1,0:T(4,128)}, u32[]{:S(2)}) copy-start(f32[3,4]{1,0:T(4,128)} %energy.1) | copy-start | bytes 148
  1.9 17.1 %collective-permute-start = (f32[4,6,16,128]{3,2,1,0:T(8,128)S(1)}, f32[4,6,16,128]{3,2,1,0:T(8,128)S(1)}, u32[]{:S(2)}, u32[]{:S(2)}) collective-permute-start(f32[4,6,16,128]{3,2,1,0:T(8,128)S(1)} %get-tuple-element.24), channel_id=1, source_target_pairs={{0,4},{4,0},{8,12},{12,8},{16,20},{20,16},{24,28},{28,24},{32,36},... | collective-permute-start | bytes 589832 | tf_op jit(solution)/shard_map/ppermute | solution.py:458
  4.0 10.4 %copy-start.5 = (s32[16]{0:T(128)S(1)}, s32[16]{0:T(128)}, u32[]{:S(2)}) copy-start(s32[16]{0:T(128)} %species.1) | copy-start | bytes 196
  4.0 15.1 %collective-permute-start.1 = (f32[4,6,16,128]{3,2,1,0:T(8,128)S(1)}, f32[4,6,16,128]{3,2,1,0:T(8,128)S(1)}, u32[]{:S(2)}, u32[]{:S(2)}) collective-permute-start(f32[4,6,16,128]{3,2,1,0:T(8,128)S(1)} %get-tuple-element.25), channel_id=1, source_target_pairs={{0,252},{4,8},{8,4},{12,16},{16,12},{20,24},{24,20},{28,32},{32,28... | collective-permute-start | bytes 589832 | tf_op jit(solution)/shard_map/ppermute | solution.py:457
  19.0 9.6 %collective-permute-start.2 = (f32[4,6,16,128]{3,2,1,0:T(8,128)S(1)}, f32[4,6,16,128]{3,2,1,0:T(8,128)S(1)}, u32[]{:S(2)}, u32[]{:S(2)}) collective-permute-start(f32[4,6,16,128]{3,2,1,0:T(8,128)S(1)} %shard_map.88.near), channel_id=1, source_target_pairs={{0,4},{4,0},{8,12},{12,8},{16,20},{20,16},{24,28},{28,24},{32,36},... | collective-permute-start | bytes 589832 | tf_op jit(solution)/shard_map/ppermute | solution.py:477
  19.2 13.3 %collective-permute-start.6 = (f32[4,6,16,128]{3,2,1,0:T(8,128)S(1)}, f32[4,6,16,128]{3,2,1,0:T(8,128)S(1)}, u32[]{:S(2)}, u32[]{:S(2)}) collective-permute-start(f32[4,6,16,128]{3,2,1,0:T(8,128)S(1)} %shard_map.89.far), channel_id=1, source_target_pairs={{0,252},{4,8},{8,4},{12,16},{16,12},{20,24},{24,20},{28,32},{32,28... | collective-permute-start | bytes 589832 | tf_op jit(solution)/shard_map/ppermute | solution.py:479
  28.7 6.4 %collective-permute-start.3 = (f32[4,5,8,128]{3,2,1,0:T(8,128)S(1)}, f32[4,5,8,128]{3,2,1,0:T(8,128)S(1)}, u32[]{:S(2)}, u32[]{:S(2)}) collective-permute-start(f32[4,5,8,128]{3,2,1,0:T(8,128)S(1)} %get-tuple-element.26), channel_id=1, source_target_pairs={{0,2},{1,3},{2,0},{3,1},{4,6},{5,7},{6,4},{7,5},{8,10},{9,11},{10,... | collective-permute-start | bytes 245768 | tf_op jit(solution)/shard_map/ppermute | solution.py:493
  29.2 8.3 %collective-permute-start.4 = (f32[4,5,8,128]{3,2,1,0:T(8,128)S(1)}, f32[4,5,8,128]{3,2,1,0:T(8,128)S(1)}, u32[]{:S(2)}, u32[]{:S(2)}) collective-permute-start(f32[4,5,8,128]{3,2,1,0:T(8,128)S(1)} %get-tuple-element.27), channel_id=1, source_target_pairs={{0,3},{1,2},{2,1},{3,0},{4,7},{5,6},{6,5},{7,4},{8,11},{9,10},{10,... | collective-permute-start | bytes 245768 | tf_op jit(solution)/shard_map/ppermute | solution.py:493
  32.5 4.9 %collective-permute-start.5 = (f32[4,5,8,128]{3,2,1,0:T(8,128)S(1)}, f32[4,5,8,128]{3,2,1,0:T(8,128)S(1)}, u32[]{:S(2)}, u32[]{:S(2)}) collective-permute-start(f32[4,5,8,128]{3,2,1,0:T(8,128)S(1)} %get-tuple-element.28), channel_id=1, source_target_pairs={{0,1},{1,0},{2,3},{3,2},{4,5},{5,4},{6,7},{7,6},{8,9},{9,8},{10,11... | collective-permute-start | bytes 245768 | tf_op jit(solution)/shard_map/ppermute | solution.py:493
  32.6 6.6 %collective-permute-start.7 = (f32[4,3,8,128]{3,2,1,0:T(8,128)S(1)}, f32[4,3,8,128]{3,2,1,0:T(8,128)S(1)}, u32[]{:S(2)}, u32[]{:S(2)}) collective-permute-start(f32[4,3,8,128]{3,2,1,0:T(8,128)S(1)} %get-tuple-element.34), channel_id=1, source_target_pairs={{0,2},{1,3},{2,0},{3,1},{4,6},{5,7},{6,4},{7,5},{8,10},{9,11},{10,... | collective-permute-start | bytes 147464 | tf_op jit(solution)/shard_map/ppermute | solution.py:493
  33.3 5.9 %collective-permute-start.8 = (f32[4,3,8,128]{3,2,1,0:T(8,128)S(1)}, f32[4,3,8,128]{3,2,1,0:T(8,128)S(1)}, u32[]{:S(2)}, u32[]{:S(2)}) collective-permute-start(f32[4,3,8,128]{3,2,1,0:T(8,128)S(1)} %get-tuple-element.35), channel_id=1, source_target_pairs={{0,3},{1,2},{2,1},{3,0},{4,7},{5,6},{6,5},{7,4},{8,11},{9,10},{10,... | collective-permute-start | bytes 147464 | tf_op jit(solution)/shard_map/ppermute | solution.py:493
  35.0 4.2 %collective-permute-start.9 = (f32[4,3,8,128]{3,2,1,0:T(8,128)S(1)}, f32[4,3,8,128]{3,2,1,0:T(8,128)S(1)}, u32[]{:S(2)}, u32[]{:S(2)}) collective-permute-start(f32[4,3,8,128]{3,2,1,0:T(8,128)S(1)} %get-tuple-element.36), channel_id=1, source_target_pairs={{0,1},{1,0},{2,3},{3,2},{4,5},{5,4},{6,7},{7,6},{8,9},{9,8},{10,11... | collective-permute-start | bytes 147464 | tf_op jit(solution)/shard_map/ppermute | solution.py:493

commit v3 on v2

--- a/solution.py
+++ b/solution.py
@@ -106,6 +106,8 @@
     potential,
     index,
     projector,
+    far,
+    near,
     out,
     rowhot,
     zhot,
@@ -134,6 +136,7 @@
             total = local_layer(lambda j: v[o, j], potential[i], i, layers)
             total = total + hat[i * 16 : (i + 1) * 16, o * 128 : (o + 1) * 128]
             out[o, i] = total * (1.0 / HALF_WIDTH)
+    cut_edges(out, far, near)
 
 
 def second_kernel(
@@ -146,7 +149,7 @@
     zhot,
     near,
     far,
-    middle,
+    part,
     out,
     parts,
     picked,
@@ -154,10 +157,14 @@
     held,
 ):
     orbs, layers = v.shape[0], v.shape[1]
-    first, last = far_near_starts(layers)
-    held[:, pl.ds(first, RADIUS)] = far[...]
-    held[:, pl.ds(last, RADIUS)] = near[...]
-    held[:, RADIUS : layers - RADIUS] = middle[:, RADIUS : layers - RADIUS]
+    held[:, RADIUS : layers - RADIUS] = part[:, RADIUS : layers - RADIUS]
+
+    def edges(below, above):
+        low, high = held.at[:, :RADIUS], held.at[:, layers - RADIUS :]
+        add_below(part.at[:, :RADIUS], below, low, -0.5 / HALF_WIDTH)
+        add_above(part.at[:, layers - RADIUS :], above, high, -0.5 / HALF_WIDTH)
+
+    by_parity(edges, far, near)
     hat = nonlocal_rows(
         lambda o: held[o].reshape(256, 128),
         orbs,
@@ -217,6 +224,26 @@
     by_parity(body, low, high)
 
 
+def cut_edges(block, far, near):
+    first, last = far_near_starts(block.shape[1])
+    for o in range(block.shape[0]):
+        far[o] = block[o, pl.ds(first, RADIUS)]
+        near[o] = block[o, pl.ds(last, RADIUS)]
+
+
+def add_below(low, below, out, scale):
+    for o in range(low.shape[0]):
+        for i in range(RADIUS):
+            out[o, i] = low[o, i] + scale * from_below(below, o, i)
+
+
+def add_above(high, above, out, scale):
+    for o in range(high.shape[0]):
+        for i in range(RADIUS):
+            at = RADIUS - 1 - i
+            out[o, at] = high[o, at] + scale * from_above(above, o, i)
+
+
 def slot_strengths(species, count, energy, strength):
     channels, atoms = strength.shape[0], strength.shape[1]
     slot = lax.broadcasted_iota(jnp.int32, (atoms, 128), 0)
@@ -228,25 +255,6 @@
         strength[p] = jnp.where(live, total, 0.0)
 
 
-def first_edge(far_side, part, got, edge):
-    orbs, layers = part.shape[0], part.shape[1]
-    scale = -0.5 / HALF_WIDTH
-    odd = lax.axis_index("dom") & 1
-
-    @pl.when(odd == (0 if far_side else 1))
-    def _():
-        for o in range(orbs):
-            for i in range(RADIUS):
-                edge[o, i] = part[o, i] + scale * from_below(got, o, i)
-
-    @pl.when(odd == (1 if far_side else 0))
-    def _():
-        for o in range(orbs):
-            for i in range(RADIUS):
-                at = layers - 1 - i
-                edge[o, RADIUS - 1 - i] = part[o, at] + scale * from_above(got, o, i)
-
-
 def deal(block, chunks):
     me = lax.axis_index("orb")
     depth = chunks[0].shape[1]
@@ -256,52 +264,52 @@
             chunk[o] = block[o, pl.ds(first, depth)]
 
 
-def second_near(part, got, block, *chunks):
-    orbs, layers = part.shape[0], part.shape[1]
-    scale = -1.0 / HALF_WIDTH
+def as_halves(rows):
+    return rows.reshape(rows.shape[0], 2 * rows.shape[1], 8, 128)
+
+
+def second_near(part, v, got, block, *scratch):
+    (*chunks, halo, edge) = scratch
+    layers = part.shape[1]
+    inner = layers - RADIUS
     odd = lax.axis_index("dom") & 1
+    one, two = -0.5 / HALF_WIDTH, -1.0 / HALF_WIDTH
 
     @pl.when(odd == 0)
     def _():
-        for o in range(orbs):
-            for i in range(RADIUS, layers):
-                rows = part[o, i]
-                if i >= layers - RADIUS:
-                    rows = rows + scale * from_above(got, o, layers - 1 - i)
-                block[o, 2 * (i - RADIUS) : 2 * (i - RADIUS) + 2] = rows.reshape(2, 8, 128)
+        add_below(got, v.at[:, inner:], halo, one)
+        add_above(part.at[:, inner:], halo, edge, two)
+        block[:, : 2 * (inner - RADIUS)] = as_halves(part[:, RADIUS:inner])
+        block[:, 2 * (inner - RADIUS) :] = as_halves(edge[...])
 
     @pl.when(odd == 1)
     def _():
-        for o in range(orbs):
-            for i in range(layers - RADIUS):
-                rows = part[o, i]
-                if i < RADIUS:
-                    rows = rows + scale * from_below(got, o, i)
-                block[o, 2 * i : 2 * i + 2] = rows.reshape(2, 8, 128)
+        add_above(got, v.at[:, :RADIUS], halo, one)
+        add_below(part.at[:, :RADIUS], halo, edge, two)
+        block[:, : 2 * RADIUS] = as_halves(edge[...])
+        block[:, 2 * RADIUS :] = as_halves(part[:, RADIUS:inner])
 
     deal(block, chunks)
 
 
-def second_far(part, got, block, *chunks):
-    orbs, layers = part.shape[0], part.shape[1]
-    scale = -1.0 / HALF_WIDTH
+def second_far(part, v, got, block, *scratch):
+    (*chunks, halo, edge) = scratch
+    layers = part.shape[1]
+    inner = layers - RADIUS
     odd = lax.axis_index("dom") & 1
+    one, two = -0.5 / HALF_WIDTH, -1.0 / HALF_WIDTH
 
     @pl.when(odd == 0)
     def _():
-        for o in range(orbs):
-            for i in range(RADIUS):
-                rows = part[o, i] + scale * from_below(got, o, i)
-                block[o, 2 * i : 2 * i + 2] = rows.reshape(2, 8, 128)
+        add_above(got, v.at[:, :RADIUS], halo, one)
+        add_below(part.at[:, :RADIUS], halo, edge, two)
 
     @pl.when(odd == 1)
     def _():
-        for o in range(orbs):
-            for i in range(RADIUS):
-                rows = part[o, layers - 1 - i] + scale * from_above(got, o, i)
-                at = 2 * (RADIUS - 1 - i)
-                block[o, at : at + 2] = rows.reshape(2, 8, 128)
-
+        add_below(got, v.at[:, inner:], halo, one)
+        add_above(part.at[:, inner:], halo, edge, two)
+
+    block[...] = as_halves(edge[...])
     deal(block, chunks)
 
 
@@ -461,9 +469,11 @@
         pltpu.VMEM((orbs,) + sphere_index.shape, f32),
         pltpu.VMEM((2, orbs * deep, atoms * points), jnp.bfloat16),
     ]
-    part, rowhot, zhot, strength = call(
+    far, near, part, rowhot, zhot, strength = call(
         first_kernel,
         (
+            edge,
+            edge,
             block,
             jax.ShapeDtypeStruct((layers * wide, atoms * points), jnp.bfloat16),
             jax.ShapeDtypeStruct((deep, atoms * points), jnp.bfloat16),
@@ -473,17 +483,15 @@
         scratch,
         flops=3_000_000_000,
     )(*scalars, *fields)
-    near = call(functools.partial(first_edge, False), edge, [in_vmem] * 2)(part, got_near)
-    got_near = lax.ppermute(near, "dom", near_pairs)
-    far = call(functools.partial(first_edge, True), edge, [in_vmem] * 2)(part, got_far)
-    got_far = lax.ppermute(far, "dom", far_pairs)
+    next_far = lax.ppermute(far, "dom", far_pairs)
+    next_near = lax.ppermute(near, "dom", near_pairs)
     part = call(
         second_kernel,
         block,
         [in_vmem] * 10,
         scratch + [pltpu.VMEM(orbitals.shape, f32)],
         flops=3_000_000_000,
-    )(*fields, strength, rowhot, zhot, near, far, part)
+    )(*fields, strength, rowhot, zhot, got_near, got_far, part)
 
     def halves(count):
         return jax.ShapeDtypeStruct((orbs, 2 * count, wide // 2, deep), f32)
@@ -502,13 +510,14 @@
 
     row = jax.ShapeDtypeStruct((1, 128), f32)
     inner = layers - RADIUS
-    near, *sends = call(second_near, (halves(inner),) + (chunk(inner),) * 4, [in_vmem] * 2)(
-        part, got_near
-    )
+    edges = [pltpu.VMEM(edge.shape, f32)] * 2
+    near, *sends = call(
+        second_near, (halves(inner),) + (chunk(inner),) * 4, [in_vmem] * 3, edges
+    )(part, orbitals, next_near)
     own_near, got_early = sends[0], swap(sends)
-    far, *sends = call(second_far, (halves(RADIUS),) + (chunk(RADIUS),) * 4, [in_vmem] * 2)(
-        part, got_far
-    )
+    far, *sends = call(
+        second_far, (halves(RADIUS),) + (chunk(RADIUS),) * 4, [in_vmem] * 3, edges
+    )(part, orbitals, next_far)
     own_far, got_late = sends[0], swap(sends)
     early = call(near_gram, row, [in_vmem] * 4, rows_of(own_near), flops=1_000_000_000)(
         got_early[2], got_early[3], got_early[1], own_near

time: 60.1 us -> 56.6 us (0.942)
  starting transfers between devices: 25.1 us -> 20.9 us
  waiting for transfers between devices: 1.38 us -> 3.46 us
  blocking collectives: 19.4 us -> 18 us
    ppermute x2 -> x1, starting transfers between devices: 15.6 us -> 9.74 us  [on_device(): got_far = lax.ppermute(far, 'dom', far_pairs)]
    ppermute x0 -> x2, waiting for transfers between devices: none -> 2.37 us  [the longest x1 1.8 us: on_device(): next_far = lax.ppermute(far, 'dom', far_pairs)]
    all_to_all x1, blocking collectives: 19.4 us -> 18 us  [on_device(): terms = lax.all_to_all(terms, ('dom', 'orb'), 0, 0)]
    ppermute x0 -> x2, starting transfers between devices: none -> 1 us  [the longest x1 0.9 us: on_device(): next_far = lax.ppermute(far, 'dom', far_pairs)]
    ppermute x6, starting transfers between devices: 7.33 us -> 8.03 us  [swap(): lax.ppermute(chunks[k], 'orb', [(i, i ^ k) for i in range(orb_devices)])]
    ppermute x2 -> x1, starting transfers between devices: 2.22 us -> 2.13 us  [on_device(): got_near = lax.ppermute(near, 'dom', near_pairs)]
    pallas_call x5 -> x3, Pallas kernels: 4.81 us -> 4.8 us  [the longest x1 4.52 us: on_device(): call(first_kernel, (edge, edge, block, jax.ShapeDtypeStruct((layers * wid...]
  transfers between devices with their start and end apart: 10 -> 10, of which waited for: 1 -> 3; matrix products, arithmetic and copies ran while one was open for 0% -> 0% of each run, Pallas kernels for 17% -> 18%
where the time goes in v3:
time: 56.6 us; the launch traced here: 56.5 us
  starting transfers between devices  20.9 us (37%)
  blocking collectives  18 us (32%)
  Pallas kernels  11.6 us (20%)
  waiting for transfers between devices  3.46 us (6%)
  between operations  1.44 us (3%)
  local copies, waits for them, and re-layouts  1.14 us (2%)
    all_to_all x1, blocking collectives, on_device(): terms = lax.all_to_all(terms, ('dom', 'orb'), 0, 0)  18 us
    ppermute x1, starting transfers between devices, on_device(): got_far = lax.ppermute(far, 'dom', far_pairs)  9.74 us
    ppermute x6, starting transfers between devices, swap(): lax.ppermute(chunks[k], 'orb', [(i, i ^ k) for i in range(orb_devices)])  8.03 us
    pallas_call x1, Pallas kernels, on_device(): call(first_kernel, (edge, edge, block, jax.ShapeDtypeStruct((layers * wid...  4.52 us
    pallas_call x1, Pallas kernels, on_device(): call(second_kernel, block, [in_vmem] * 10, scratch + [pltpu.VMEM(orbitals...  3.66 us
    ppermute x1, starting transfers between devices, on_device(): got_near = lax.ppermute(near, 'dom', near_pairs)  2.13 us
    ppermute x1, waiting for transfers between devices, on_device(): next_far = lax.ppermute(far, 'dom', far_pairs)  1.8 us
    pallas_call x1, Pallas kernels, on_device(): call(own_gram, (block, row), [in_vmem] * 3, flops=1500000000)  1.24 us
  transfers between devices with their start and end apart: 10, of which 3 were waited for; matrix products, arithmetic and copies ran while one was open for 0% of the time, Pallas kernels for 18%

profile of v3, /device:TPU:1, one launch (start us, length us, event | category | flops | bytes accessed | tf_op | source)
XLA Modules:
  0.0 56.5 jit_solution(11743559903501238522)
XLA Ops:
  0.6 1.1 %fusion = (f32[4,6,16,128]{3,2,1,0:T(8,128)S(1)}, f32[4,6,16,128]{3,2,1,0:T(8,128)S(1)}) fusion(f32[4,16,16,128]{3,2,1,0:T(8,128)} %v.7), kind=kLoop, calls=%fused_computation | loop fusion | bytes 786432 | tf_op jit(solution)/shard_map/slice | solution.py:463
  1.8 0.0 copy-start.1
  1.8 0.0 copy-start.2
  1.8 0.0 copy-start.3
  1.8 0.0 copy-start.4
  1.9 2.1 %collective-permute-start = (f32[4,6,16,128]{3,2,1,0:T(8,128)S(1)}, f32[4,6,16,128]{3,2,1,0:T(8,128)S(1)}, u32[]{:S(2)}, u32[]{:S(2)}) collective-permute-start(f32[4,6,16,128]{3,2,1,0:T(8,128)S(1)} %get-tuple-element.25), channel_id=1, source_target_pairs={{0,4},{4,0},{8,12},{12,8},{16,20},{20,16},{24,28},{28,24},{32,36},... | collective-permute-start | bytes 589832 | tf_op jit(solution)/shard_map/ppermute | solution.py:466
  4.0 9.7 %collective-permute-start.1 = (f32[4,6,16,128]{3,2,1,0:T(8,128)S(1)}, f32[4,6,16,128]{3,2,1,0:T(8,128)S(1)}, u32[]{:S(2)}, u32[]{:S(2)}) collective-permute-start(f32[4,6,16,128]{3,2,1,0:T(8,128)S(1)} %get-tuple-element.26), channel_id=1, source_target_pairs={{0,252},{4,8},{8,4},{12,16},{16,12},{20,24},{24,20},{28,32},{32,28... | collective-permute-start | bytes 589832 | tf_op jit(solution)/shard_map/ppermute | solution.py:465
  14.4 4.5 %shard_map.86 = (f32[4,6,16,128]{3,2,1,0:T(8,128)S(1)}, f32[4,6,16,128]{3,2,1,0:T(8,128)S(1)}, f32[4,16,16,128]{3,2,1,0:T(8,128)S(1)}, bf16[256,2048]{1,0:T(8,12...) custom-call(s32[16]{0:T(128)S(1)} %copy-done.5, s32[1]{0:T(128)S(6)} %copy.9.count, ...), custom_call_target="tpu_custom_call" | custom-call | flops 3000000000 | bytes 2097152 | tf_op jit(solution)/shard_map/pallas_call | solution.py:472
  18.9 0.1 collective-permute-start.2
  19.1 0.9 %collective-permute-start.6 = (f32[4,6,16,128]{3,2,1,0:T(8,128)S(1)}, f32[4,6,16,128]{3,2,1,0:T(8,128)S(1)}, u32[]{:S(2)}, u32[]{:S(2)}) collective-permute-start(f32[4,6,16,128]{3,2,1,0:T(8,128)S(1)} %get-tuple-element.34), channel_id=1, source_target_pairs={{0,252},{4,8},{8,4},{12,16},{16,12},{20,24},{24,20},{28,32},{32,28... | collective-permute-start | bytes 589832 | tf_op jit(solution)/shard_map/ppermute | solution.py:486
  20.0 0.0 collective-permute-done.near
  20.0 0.0 collective-permute-done.1.far
  20.0 3.7 %shard_map.88.part = f32[4,16,16,128]{3,2,1,0:T(8,128)S(1)} custom-call(f32[4,16,16,128]{3,2,1,0:T(8,128)S(1)} %copy-done, f32[16,16,128]{2,1,0:T(8,128)S(1)} %copy-done.1, s32[16,128]{1,0:T(8,128)S(1)} %copy-done.3, f32[16,4,128]{2,1,0:T(4,128)S(1)} %copy-done.2, f32[4,16,128]{2,1,0:T(8,128)S(1)} %get-tuple-element.22.strength, ...), custom_call_target="tpu_custom_call" | custom-call | flops 3000000000 | bytes 2097152 | tf_op jit(solution)/shard_map/pallas_call | solution.py:488
  23.6 0.6 %collective-permute-done.2.got = f32[4,6,16,128]{3,2,1,0:T(8,128)S(1)} collective-permute-done((f32[4,6,16,128]{3,2,1,0:T(8,128)S(1)}, f32[4,6,16,128]{3,2,1,0:T(8,128)S(1)}, u32[]{:S(2)}, u32[]{:S(2)}) %collective-permute-start.2) | collective-permute-done | bytes 196640 | tf_op jit(solution)/shard_map/ppermute | solution.py:487
  24.2 0.1 shard_map.89
  24.4 0.5 collective-permute-start.3
  24.8 3.4 %collective-permute-start.4 = (f32[4,5,8,128]{3,2,1,0:T(8,128)S(1)}, f32[4,5,8,128]{3,2,1,0:T(8,128)S(1)}, u32[]{:S(2)}, u32[]{:S(2)}) collective-permute-start(f32[4,5,8,128]{3,2,1,0:T(8,128)S(1)} %get-tuple-element.30), channel_id=1, source_target_pairs={{0,3},{1,2},{2,1},{3,0},{4,7},{5,6},{6,5},{7,4},{8,11},{9,10},{10,... | collective-permute-start | bytes 245768 | tf_op jit(solution)/shard_map/ppermute | solution.py:501
  28.2 0.0 collective-permute-start.5
  28.2 1.8 %collective-permute-done.6.got = f32[4,6,16,128]{3,2,1,0:T(8,128)S(1)} collective-permute-done((f32[4,6,16,128]{3,2,1,0:T(8,128)S(1)}, f32[4,6,16,128]{3,2,1,0:T(8,128)S(1)}, u32[]{:S(2)}, u32[]{:S(2)}) %collective-permute-start.6) | collective-permute-done | bytes 196640 | tf_op jit(solution)/shard_map/ppermute | solution.py:486
  30.0 0.1 shard_map.91
  30.2 0.7 %collective-permute-start.7 = (f32[4,3,8,128]{3,2,1,0:T(8,128)S(1)}, f32[4,3,8,128]{3,2,1,0:T(8,128)S(1)}, u32[]{:S(2)}, u32[]{:S(2)}) collective-permute-start(f32[4,3,8,128]{3,2,1,0:T(8,128)S(1)} %get-tuple-element.38), channel_id=1, source_target_pairs={{0,2},{1,3},{2,0},{3,1},{4,6},{5,7},{6,4},{7,5},{8,10},{9,11},{10,... | collective-permute-start | bytes 147464 | tf_op jit(solution)/shard_map/ppermute | solution.py:501
  30.8 3.5 %collective-permute-start.8 = (f32[4,3,8,128]{3,2,1,0:T(8,128)S(1)}, f32[4,3,8,128]{3,2,1,0:T(8,128)S(1)}, u32[]{:S(2)}, u32[]{:S(2)}) collective-permute-start(f32[4,3,8,128]{3,2,1,0:T(8,128)S(1)} %get-tuple-element.39), channel_id=1, source_target_pairs={{0,3},{1,2},{2,1},{3,0},{4,7},{5,6},{6,5},{7,4},{8,11},{9,10},{10,... | collective-permute-start | bytes 147464 | tf_op jit(solution)/shard_map/ppermute | solution.py:501
  34.3 0.0 collective-permute-done.3.got_2
  34.3 0.0 collective-permute-start.9
  34.3 0.0 collective-permute-done.4.got_3
  34.4 0.5 shard_map.90.early
  34.8 1.2 %shard_map.92 = (f32[4,16,16,128]{3,2,1,0:T(8,128)}, f32[1,128]{1,0:T(1,128)S(1)}) custom-call(f32[1,128]{1,0:T(1,128)S(1)} %shard_map.90.early, f32[4,20,8,128]{3,2,1,0:T(8,128)S(1)} %get-tuple-element.33.near, f32[4,12,8,128]{3,2,1,0:T(8,128)S(1)} %get-tuple-element.35.far), custom_call_target="tpu_custom_call" | custom-call | flops 1500000000 | bytes 2097152 | tf_op jit(solution)/shard_map/pallas_call | solution.py:525
  36.1 0.0 collective-permute-done.7.got_2
  36.1 1.1 %collective-permute-done.8.got_3 = f32[4,3,8,128]{3,2,1,0:T(8,128)S(1)} collective-permute-done((f32[4,3,8,128]{3,2,1,0:T(8,128)S(1)}, f32[4,3,8,128]{3,2,1,0:T(8,128)S(1)}, u32[]{:S(2)}, u32[]{:S(2)}) %collective-permute-start.8) | collective-permute-done | bytes 49184 | tf_op jit(solution)/shard_map/ppermute | solution.py:501
  37.2 0.5 shard_map.93
  37.6 18.0 %all_to_all.5.terms = f32[256,1,128]{2,1,0:T(1,128)S(1)} all-to-all(f32[256,1,128]{2,1,0:T(1,128)S(1)} %shard_map.93), channel_id=1, replica_groups=mesh['dom'=64,'orb'=4] {'dom','orb'}, dimensions={0} | all-to-all | bytes 262144 | tf_op jit(solution)/shard_map/all_to_all | solution.py:534
  55.6 0.9 %shard_map.94 = f32[16,16]{1,0:T(8,128)} custom-call(f32[256,1,128]{2,1,0:T(1,128)S(1)} %all_to_all.5.terms), custom_call_target="tpu_custom_call" | custom-call | flops 10000000 | bytes 2097152 | tf_op jit(solution)/shard_map/pallas_call | solution.py:535
  (11 shorter events, 0.1 us)
Async XLA Ops:
  0.6 13.7 %copy-start = (f32[4,16,16,128]{3,2,1,0:T(8,128)S(1)}, f32[4,16,16,128]{3,2,1,0:T(8,128)}, u32[]{:S(2)}) copy-start(f32[4,16,16,128]{3,2,1,0:T(8,128)} %v.7) | copy-start | bytes 1572868
  1.8 12.6 %copy-start.1 = (f32[16,16,128]{2,1,0:T(8,128)S(1)}, f32[16,16,128]{2,1,0:T(8,128)}, u32[]{:S(2)}) copy-start(f32[16,16,128]{2,1,0:T(8,128)} %potential.3) | copy-start | bytes 393220
  1.8 12.6 %copy-start.2 = (f32[16,4,128]{2,1,0:T(4,128)S(1)}, f32[16,4,128]{2,1,0:T(4,128)}, u32[]{:S(2)}) copy-start(f32[16,4,128]{2,1,0:T(4,128)} %projector.3) | copy-start | bytes 98308
  1.8 12.6 %copy-start.3 = (s32[16,128]{1,0:T(8,128)S(1)}, s32[16,128]{1,0:T(8,128)}, u32[]{:S(2)}) copy-start(s32[16,128]{1,0:T(8,128)} %index.3) | copy-start | bytes 24580
  1.8 12.6 %copy-start.4 = (f32[3,4]{1,0:T(4,128)S(1)}, f32[3,4]{1,0:T(4,128)}, u32[]{:S(2)}) copy-start(f32[3,4]{1,0:T(4,128)} %energy.1) | copy-start | bytes 148
  1.9 18.1 %collective-permute-start = (f32[4,6,16,128]{3,2,1,0:T(8,128)S(1)}, f32[4,6,16,128]{3,2,1,0:T(8,128)S(1)}, u32[]{:S(2)}, u32[]{:S(2)}) collective-permute-start(f32[4,6,16,128]{3,2,1,0:T(8,128)S(1)} %get-tuple-element.25), channel_id=1, source_target_pairs={{0,4},{4,0},{8,12},{12,8},{16,20},{20,16},{24,28},{28,24},{32,36},... | collective-permute-start | bytes 589832 | tf_op jit(solution)/shard_map/ppermute | solution.py:466
  4.0 10.4 %copy-start.5 = (s32[16]{0:T(128)S(1)}, s32[16]{0:T(128)}, u32[]{:S(2)}) copy-start(s32[16]{0:T(128)} %species.1) | copy-start | bytes 196
  4.0 16.0 %collective-permute-start.1 = (f32[4,6,16,128]{3,2,1,0:T(8,128)S(1)}, f32[4,6,16,128]{3,2,1,0:T(8,128)S(1)}, u32[]{:S(2)}, u32[]{:S(2)}) collective-permute-start(f32[4,6,16,128]{3,2,1,0:T(8,128)S(1)} %get-tuple-element.26), channel_id=1, source_target_pairs={{0,252},{4,8},{8,4},{12,16},{16,12},{20,24},{24,20},{28,32},{32,28... | collective-permute-start | bytes 589832 | tf_op jit(solution)/shard_map/ppermute | solution.py:465
  18.9 5.3 %collective-permute-start.2 = (f32[4,6,16,128]{3,2,1,0:T(8,128)S(1)}, f32[4,6,16,128]{3,2,1,0:T(8,128)S(1)}, u32[]{:S(2)}, u32[]{:S(2)}) collective-permute-start(f32[4,6,16,128]{3,2,1,0:T(8,128)S(1)} %get-tuple-element.28), channel_id=1, source_target_pairs={{0,4},{4,0},{8,12},{12,8},{16,20},{20,16},{24,28},{28,24},{32,36},... | collective-permute-start | bytes 589832 | tf_op jit(solution)/shard_map/ppermute | solution.py:487
  19.1 11.0 %collective-permute-start.6 = (f32[4,6,16,128]{3,2,1,0:T(8,128)S(1)}, f32[4,6,16,128]{3,2,1,0:T(8,128)S(1)}, u32[]{:S(2)}, u32[]{:S(2)}) collective-permute-start(f32[4,6,16,128]{3,2,1,0:T(8,128)S(1)} %get-tuple-element.34), channel_id=1, source_target_pairs={{0,252},{4,8},{8,4},{12,16},{16,12},{20,24},{24,20},{28,32},{32,28... | collective-permute-start | bytes 589832 | tf_op jit(solution)/shard_map/ppermute | solution.py:486
  24.4 10.0 %collective-permute-start.3 = (f32[4,5,8,128]{3,2,1,0:T(8,128)S(1)}, f32[4,5,8,128]{3,2,1,0:T(8,128)S(1)}, u32[]{:S(2)}, u32[]{:S(2)}) collective-permute-start(f32[4,5,8,128]{3,2,1,0:T(8,128)S(1)} %get-tuple-element.29), channel_id=1, source_target_pairs={{0,2},{1,3},{2,0},{3,1},{4,6},{5,7},{6,4},{7,5},{8,10},{9,11},{10,... | collective-permute-start | bytes 245768 | tf_op jit(solution)/shard_map/ppermute | solution.py:501
  24.8 9.5 %collective-permute-start.4 = (f32[4,5,8,128]{3,2,1,0:T(8,128)S(1)}, f32[4,5,8,128]{3,2,1,0:T(8,128)S(1)}, u32[]{:S(2)}, u32[]{:S(2)}) collective-permute-start(f32[4,5,8,128]{3,2,1,0:T(8,128)S(1)} %get-tuple-element.30), channel_id=1, source_target_pairs={{0,3},{1,2},{2,1},{3,0},{4,7},{5,6},{6,5},{7,4},{8,11},{9,10},{10,... | collective-permute-start | bytes 245768 | tf_op jit(solution)/shard_map/ppermute | solution.py:501
  28.2 6.1 %collective-permute-start.5 = (f32[4,5,8,128]{3,2,1,0:T(8,128)S(1)}, f32[4,5,8,128]{3,2,1,0:T(8,128)S(1)}, u32[]{:S(2)}, u32[]{:S(2)}) collective-permute-start(f32[4,5,8,128]{3,2,1,0:T(8,128)S(1)} %get-tuple-element.31), channel_id=1, source_target_pairs={{0,1},{1,0},{2,3},{3,2},{4,5},{5,4},{6,7},{7,6},{8,9},{9,8},{10,11... | collective-permute-start | bytes 245768 | tf_op jit(solution)/shard_map/ppermute | solution.py:501
  30.2 5.9 %collective-permute-start.7 = (f32[4,3,8,128]{3,2,1,0:T(8,128)S(1)}, f32[4,3,8,128]{3,2,1,0:T(8,128)S(1)}, u32[]{:S(2)}, u32[]{:S(2)}) collective-permute-start(f32[4,3,8,128]{3,2,1,0:T(8,128)S(1)} %get-tuple-element.38), channel_id=1, source_target_pairs={{0,2},{1,3},{2,0},{3,1},{4,6},{5,7},{6,4},{7,5},{8,10},{9,11},{10,... | collective-permute-start | bytes 147464 | tf_op jit(solution)/shard_map/ppermute | solution.py:501
  30.8 6.3 %collective-permute-start.8 = (f32[4,3,8,128]{3,2,1,0:T(8,128)S(1)}, f32[4,3,8,128]{3,2,1,0:T(8,128)S(1)}, u32[]{:S(2)}, u32[]{:S(2)}) collective-permute-start(f32[4,3,8,128]{3,2,1,0:T(8,128)S(1)} %get-tuple-element.39), channel_id=1, source_target_pairs={{0,3},{1,2},{2,1},{3,0},{4,7},{5,6},{6,5},{7,4},{8,11},{9,10},{10,... | collective-permute-start | bytes 147464 | tf_op jit(solution)/shard_map/ppermute | solution.py:501
  34.3 2.8 %collective-permute-start.9 = (f32[4,3,8,128]{3,2,1,0:T(8,128)S(1)}, f32[4,3,8,128]{3,2,1,0:T(8,128)S(1)}, u32[]{:S(2)}, u32[]{:S(2)}) collective-permute-start(f32[4,3,8,128]{3,2,1,0:T(8,128)S(1)} %get-tuple-element.40), channel_id=1, source_target_pairs={{0,1},{1,0},{2,3},{3,2},{4,5},{5,4},{6,7},{7,6},{8,9},{9,8},{10,11... | collective-permute-start | bytes 147464 | tf_op jit(solution)/shard_map/ppermute | solution.py:501

commit v4 on v3

--- a/solution.py
+++ b/solution.py
@@ -246,12 +246,17 @@
 
 def slot_strengths(species, count, energy, strength):
     channels, atoms = strength.shape[0], strength.shape[1]
+    slot = lax.broadcasted_iota(jnp.int32, (atoms, atoms), 0)
+    lane = lax.broadcasted_iota(jnp.int32, (atoms, atoms), 1)
+    kinds = species[...].astype(jnp.float32).reshape(1, atoms)
+    kinds = jnp.sum(jnp.where(slot == lane, kinds, 0.0), axis=1, keepdims=True)
+    kinds = jnp.broadcast_to(kinds, (atoms, 128))
     slot = lax.broadcasted_iota(jnp.int32, (atoms, 128), 0)
-    live = slot < count[0]
+    live = slot < count[...].reshape(1, 1)
     for p in range(channels):
         total = jnp.zeros((atoms, 128), jnp.float32)
-        for a in range(atoms):
-            total = jnp.where(slot == a, energy[species[a], p], total)
+        for kind in range(energy.shape[0]):
+            total = jnp.where(kinds == float(kind), energy[kind : kind + 1, p : p + 1], total)
         strength[p] = jnp.where(live, total, 0.0)
 
 
@@ -329,13 +334,17 @@
 
 
 def row_products(loads, rows, left_rows, right_rows):
-    total = None
+    left, right = [], []
     for load in loads:
         high, low = split(load().reshape(rows, 128))
-        left = jnp.concatenate([high, high, low], axis=1)[left_rows]
-        right = jnp.concatenate([high, low, high], axis=1)[right_rows]
-        term = lax.dot_general(left, right, NT, preferred_element_type=jnp.float32)
-        total = term if total is None else total + term
+        left += [high, high, low]
+        right += [high, low, high]
+    total = lax.dot_general(
+        jnp.concatenate(left, axis=1)[left_rows],
+        jnp.concatenate(right, axis=1)[right_rows],
+        NT,
+        preferred_element_type=jnp.float32,
+    )
     row = lax.broadcasted_iota(jnp.int32, total.shape, 0)
     column = lax.broadcasted_iota(jnp.int32, total.shape, 1)
     total = jnp.where((row & 7) == (column & 7), total, 0.0)
@@ -456,7 +465,6 @@
     edge = jax.ShapeDtypeStruct((orbs, RADIUS, wide, deep), f32)
     block = jax.ShapeDtypeStruct(orbitals.shape, f32)
     atoms, points = sphere_index.shape
-    in_smem = pl.BlockSpec(memory_space=pltpu.SMEM)
     scalars = (species, atom_count, channel_energy)
     fields = (orbitals, local_potential, sphere_index, projector)
     far, near = call(order_edges, (edge, edge), [in_vmem] * 2)(
@@ -479,7 +487,7 @@
             jax.ShapeDtypeStruct((deep, atoms * points), jnp.bfloat16),
             jax.ShapeDtypeStruct((projector.shape[1], atoms, deep), f32),
         ),
-        [in_smem] * 3 + [in_vmem] * 4,
+        [in_vmem] * 7,
         scratch,
         flops=3_000_000_000,
     )(*scalars, *fields)

time: 56.6 us -> 56.1 us (level)
  Pallas kernels: 11.6 us -> 11 us
  transfers between devices with their start and end apart: 10 -> 10, of which waited for: 3 -> 3; matrix products, arithmetic and copies ran while one was open for 0% -> 0% of each run, Pallas kernels for 18% -> 17%
where the time goes in v4:
time: 56.1 us; the launch traced here: 56 us
  starting transfers between devices  20.9 us (37%)
  blocking collectives  18 us (32%)
  Pallas kernels  11 us (20%)
  waiting for transfers between devices  3.55 us (6%)
  between operations  1.44 us (3%)
  local copies, waits for them, and re-layouts  1.14 us (2%)
    all_to_all x1, blocking collectives, on_device(): terms = lax.all_to_all(terms, ('dom', 'orb'), 0, 0)  18 us
    ppermute x1, starting transfers between devices, on_device(): got_far = lax.ppermute(far, 'dom', far_pairs)  9.74 us
    ppermute x6, starting transfers between devices, swap(): lax.ppermute(chunks[k], 'orb', [(i, i ^ k) for i in range(orb_devices)])  8.04 us
    pallas_call x1, Pallas kernels, on_device(): call(first_kernel, (edge, edge, block, jax.ShapeDtypeStruct((layers * wid...  4.07 us
    pallas_call x1, Pallas kernels, on_device(): call(second_kernel, block, [in_vmem] * 10, scratch + [pltpu.VMEM(orbitals...  3.66 us
    ppermute x1, starting transfers between devices, on_device(): got_near = lax.ppermute(near, 'dom', near_pairs)  2.13 us
    ppermute x1, waiting for transfers between devices, on_device(): next_far = lax.ppermute(far, 'dom', far_pairs)  1.79 us
    ppermute x6, waiting for transfers between devices, swap(): lax.ppermute(chunks[k], 'orb', [(i, i ^ k) for i in range(orb_devices)])  1.19 us
  transfers between devices with their start and end apart: 10, of which 3 were waited for; matrix products, arithmetic and copies ran while one was open for 0% of the time, Pallas kernels for 17%

profile of v4, /device:TPU:1, one launch (start us, length us, event | category | flops | bytes accessed | tf_op | source)
XLA Modules:
  0.0 56.0 jit_solution(14736341898526444758)
XLA Ops:
  0.6 1.1 %fusion = (f32[4,6,16,128]{3,2,1,0:T(8,128)S(1)}, f32[4,6,16,128]{3,2,1,0:T(8,128)S(1)}) fusion(f32[4,16,16,128]{3,2,1,0:T(8,128)} %v.7), kind=kLoop, calls=%fused_computation | loop fusion | bytes 786432 | tf_op jit(solution)/shard_map/slice | solution.py:471
  1.8 0.0 copy-start.1
  1.8 0.0 copy-start.2
  1.8 0.0 copy-start.3
  1.8 0.0 copy-start.4
  1.9 2.1 %collective-permute-start = (f32[4,6,16,128]{3,2,1,0:T(8,128)S(1)}, f32[4,6,16,128]{3,2,1,0:T(8,128)S(1)}, u32[]{:S(2)}, u32[]{:S(2)}) collective-permute-start(f32[4,6,16,128]{3,2,1,0:T(8,128)S(1)} %get-tuple-element.25), channel_id=1, source_target_pairs={{0,4},{4,0},{8,12},{12,8},{16,20},{20,16},{24,28},{28,24},{32,36},... | collective-permute-start | bytes 589832 | tf_op jit(solution)/shard_map/ppermute | solution.py:474
  4.0 9.7 %collective-permute-start.1 = (f32[4,6,16,128]{3,2,1,0:T(8,128)S(1)}, f32[4,6,16,128]{3,2,1,0:T(8,128)S(1)}, u32[]{:S(2)}, u32[]{:S(2)}) collective-permute-start(f32[4,6,16,128]{3,2,1,0:T(8,128)S(1)} %get-tuple-element.26), channel_id=1, source_target_pairs={{0,252},{4,8},{8,4},{12,16},{16,12},{20,24},{24,20},{28,32},{32,28... | collective-permute-start | bytes 589832 | tf_op jit(solution)/shard_map/ppermute | solution.py:473
  14.4 4.1 %shard_map.86 = (f32[4,6,16,128]{3,2,1,0:T(8,128)S(1)}, f32[4,6,16,128]{3,2,1,0:T(8,128)S(1)}, f32[4,16,16,128]{3,2,1,0:T(8,128)S(1)}, bf16[256,2048]{1,0:T(8,12...) custom-call(s32[16]{0:T(128)S(1)} %copy-done.5, s32[1]{0:T(128)S(6)} %copy.9.count, ...), custom_call_target="tpu_custom_call" | custom-call | flops 3000000000 | bytes 2097152 | tf_op jit(solution)/shard_map/pallas_call | solution.py:480
  18.5 0.1 collective-permute-start.2
  18.6 0.9 %collective-permute-start.6 = (f32[4,6,16,128]{3,2,1,0:T(8,128)S(1)}, f32[4,6,16,128]{3,2,1,0:T(8,128)S(1)}, u32[]{:S(2)}, u32[]{:S(2)}) collective-permute-start(f32[4,6,16,128]{3,2,1,0:T(8,128)S(1)} %get-tuple-element.34), channel_id=1, source_target_pairs={{0,252},{4,8},{8,4},{12,16},{16,12},{20,24},{24,20},{28,32},{32,28... | collective-permute-start | bytes 589832 | tf_op jit(solution)/shard_map/ppermute | solution.py:494
  19.5 0.0 collective-permute-done.near
  19.5 0.0 collective-permute-done.1.far
  19.5 3.7 %shard_map.88.part = f32[4,16,16,128]{3,2,1,0:T(8,128)S(1)} custom-call(f32[4,16,16,128]{3,2,1,0:T(8,128)S(1)} %copy-done, f32[16,16,128]{2,1,0:T(8,128)S(1)} %copy-done.1, s32[16,128]{1,0:T(8,128)S(1)} %copy-done.3, f32[16,4,128]{2,1,0:T(4,128)S(1)} %copy-done.2, f32[4,16,128]{2,1,0:T(8,128)S(1)} %get-tuple-element.22.strength, ...), custom_call_target="tpu_custom_call" | custom-call | flops 3000000000 | bytes 2097152 | tf_op jit(solution)/shard_map/pallas_call | solution.py:496
  23.2 0.6 collective-permute-done.2.got
  23.7 0.1 shard_map.89
  23.9 0.5 collective-permute-start.3
  24.4 3.4 %collective-permute-start.4 = (f32[4,5,8,128]{3,2,1,0:T(8,128)S(1)}, f32[4,5,8,128]{3,2,1,0:T(8,128)S(1)}, u32[]{:S(2)}, u32[]{:S(2)}) collective-permute-start(f32[4,5,8,128]{3,2,1,0:T(8,128)S(1)} %get-tuple-element.30), channel_id=1, source_target_pairs={{0,3},{1,2},{2,1},{3,0},{4,7},{5,6},{6,5},{7,4},{8,11},{9,10},{10,... | collective-permute-start | bytes 245768 | tf_op jit(solution)/shard_map/ppermute | solution.py:509
  27.8 0.0 collective-permute-start.5
  27.8 1.8 %collective-permute-done.6.got = f32[4,6,16,128]{3,2,1,0:T(8,128)S(1)} collective-permute-done((f32[4,6,16,128]{3,2,1,0:T(8,128)S(1)}, f32[4,6,16,128]{3,2,1,0:T(8,128)S(1)}, u32[]{:S(2)}, u32[]{:S(2)}) %collective-permute-start.6) | collective-permute-done | bytes 196640 | tf_op jit(solution)/shard_map/ppermute | solution.py:494
  29.6 0.1 shard_map.91
  29.7 0.7 %collective-permute-start.7 = (f32[4,3,8,128]{3,2,1,0:T(8,128)S(1)}, f32[4,3,8,128]{3,2,1,0:T(8,128)S(1)}, u32[]{:S(2)}, u32[]{:S(2)}) collective-permute-start(f32[4,3,8,128]{3,2,1,0:T(8,128)S(1)} %get-tuple-element.38), channel_id=1, source_target_pairs={{0,2},{1,3},{2,0},{3,1},{4,6},{5,7},{6,4},{7,5},{8,10},{9,11},{10,... | collective-permute-start | bytes 147464 | tf_op jit(solution)/shard_map/ppermute | solution.py:509
  30.4 3.5 %collective-permute-start.8 = (f32[4,3,8,128]{3,2,1,0:T(8,128)S(1)}, f32[4,3,8,128]{3,2,1,0:T(8,128)S(1)}, u32[]{:S(2)}, u32[]{:S(2)}) collective-permute-start(f32[4,3,8,128]{3,2,1,0:T(8,128)S(1)} %get-tuple-element.39), channel_id=1, source_target_pairs={{0,3},{1,2},{2,1},{3,0},{4,7},{5,6},{6,5},{7,4},{8,11},{9,10},{10,... | collective-permute-start | bytes 147464 | tf_op jit(solution)/shard_map/ppermute | solution.py:509
  33.9 0.0 collective-permute-done.3.got_2
  33.9 0.0 collective-permute-start.9
  33.9 0.0 collective-permute-done.4.got_3
  33.9 0.4 shard_map.90.early
  34.3 1.2 %shard_map.92 = (f32[4,16,16,128]{3,2,1,0:T(8,128)}, f32[1,128]{1,0:T(1,128)S(1)}) custom-call(f32[1,128]{1,0:T(1,128)S(1)} %shard_map.90.early, f32[4,20,8,128]{3,2,1,0:T(8,128)S(1)} %get-tuple-element.33.near, f32[4,12,8,128]{3,2,1,0:T(8,128)S(1)} %get-tuple-element.35.far), custom_call_target="tpu_custom_call" | custom-call | flops 1500000000 | bytes 2097152 | tf_op jit(solution)/shard_map/pallas_call | solution.py:533
  35.5 0.0 collective-permute-done.7.got_2
  35.5 1.2 %collective-permute-done.8.got_3 = f32[4,3,8,128]{3,2,1,0:T(8,128)S(1)} collective-permute-done((f32[4,3,8,128]{3,2,1,0:T(8,128)S(1)}, f32[4,3,8,128]{3,2,1,0:T(8,128)S(1)}, u32[]{:S(2)}, u32[]{:S(2)}) %collective-permute-start.8) | collective-permute-done | bytes 49184 | tf_op jit(solution)/shard_map/ppermute | solution.py:509
  36.7 0.5 shard_map.93
  37.2 18.0 %all_to_all.5.terms = f32[256,1,128]{2,1,0:T(1,128)S(1)} all-to-all(f32[256,1,128]{2,1,0:T(1,128)S(1)} %shard_map.93), channel_id=1, replica_groups=mesh['dom'=64,'orb'=4] {'dom','orb'}, dimensions={0} | all-to-all | bytes 262144 | tf_op jit(solution)/shard_map/all_to_all | solution.py:542
  55.2 0.9 %shard_map.94 = f32[16,16]{1,0:T(8,128)} custom-call(f32[256,1,128]{2,1,0:T(1,128)S(1)} %all_to_all.5.terms), custom_call_target="tpu_custom_call" | custom-call | flops 10000000 | bytes 2097152 | tf_op jit(solution)/shard_map/pallas_call | solution.py:543
  (11 shorter events, 0.1 us)
Async XLA Ops:
  0.6 13.7 %copy-start = (f32[4,16,16,128]{3,2,1,0:T(8,128)S(1)}, f32[4,16,16,128]{3,2,1,0:T(8,128)}, u32[]{:S(2)}) copy-start(f32[4,16,16,128]{3,2,1,0:T(8,128)} %v.7) | copy-start | bytes 1572868
  1.8 12.6 %copy-start.1 = (f32[16,16,128]{2,1,0:T(8,128)S(1)}, f32[16,16,128]{2,1,0:T(8,128)}, u32[]{:S(2)}) copy-start(f32[16,16,128]{2,1,0:T(8,128)} %potential.3) | copy-start | bytes 393220
  1.8 12.6 %copy-start.2 = (f32[16,4,128]{2,1,0:T(4,128)S(1)}, f32[16,4,128]{2,1,0:T(4,128)}, u32[]{:S(2)}) copy-start(f32[16,4,128]{2,1,0:T(4,128)} %projector.3) | copy-start | bytes 98308
  1.8 12.6 %copy-start.3 = (s32[16,128]{1,0:T(8,128)S(1)}, s32[16,128]{1,0:T(8,128)}, u32[]{:S(2)}) copy-start(s32[16,128]{1,0:T(8,128)} %index.3) | copy-start | bytes 24580
  1.8 12.6 %copy-start.4 = (f32[3,4]{1,0:T(4,128)S(1)}, f32[3,4]{1,0:T(4,128)}, u32[]{:S(2)}) copy-start(f32[3,4]{1,0:T(4,128)} %energy.1) | copy-start | bytes 148
  1.9 17.7 %collective-permute-start = (f32[4,6,16,128]{3,2,1,0:T(8,128)S(1)}, f32[4,6,16,128]{3,2,1,0:T(8,128)S(1)}, u32[]{:S(2)}, u32[]{:S(2)}) collective-permute-start(f32[4,6,16,128]{3,2,1,0:T(8,128)S(1)} %get-tuple-element.25), channel_id=1, source_target_pairs={{0,4},{4,0},{8,12},{12,8},{16,20},{20,16},{24,28},{28,24},{32,36},... | collective-permute-start | bytes 589832 | tf_op jit(solution)/shard_map/ppermute | solution.py:474
  4.0 10.4 %copy-start.5 = (s32[16]{0:T(128)S(1)}, s32[16]{0:T(128)}, u32[]{:S(2)}) copy-start(s32[16]{0:T(128)} %species.1) | copy-start | bytes 196
  4.0 15.5 %collective-permute-start.1 = (f32[4,6,16,128]{3,2,1,0:T(8,128)S(1)}, f32[4,6,16,128]{3,2,1,0:T(8,128)S(1)}, u32[]{:S(2)}, u32[]{:S(2)}) collective-permute-start(f32[4,6,16,128]{3,2,1,0:T(8,128)S(1)} %get-tuple-element.26), channel_id=1, source_target_pairs={{0,252},{4,8},{8,4},{12,16},{16,12},{20,24},{24,20},{28,32},{32,28... | collective-permute-start | bytes 589832 | tf_op jit(solution)/shard_map/ppermute | solution.py:473
  18.5 5.2 %collective-permute-start.2 = (f32[4,6,16,128]{3,2,1,0:T(8,128)S(1)}, f32[4,6,16,128]{3,2,1,0:T(8,128)S(1)}, u32[]{:S(2)}, u32[]{:S(2)}) collective-permute-start(f32[4,6,16,128]{3,2,1,0:T(8,128)S(1)} %get-tuple-element.28), channel_id=1, source_target_pairs={{0,4},{4,0},{8,12},{12,8},{16,20},{20,16},{24,28},{28,24},{32,36},... | collective-permute-start | bytes 589832 | tf_op jit(solution)/shard_map/ppermute | solution.py:495
  18.6 11.0 %collective-permute-start.6 = (f32[4,6,16,128]{3,2,1,0:T(8,128)S(1)}, f32[4,6,16,128]{3,2,1,0:T(8,128)S(1)}, u32[]{:S(2)}, u32[]{:S(2)}) collective-permute-start(f32[4,6,16,128]{3,2,1,0:T(8,128)S(1)} %get-tuple-element.34), channel_id=1, source_target_pairs={{0,252},{4,8},{8,4},{12,16},{16,12},{20,24},{24,20},{28,32},{32,28... | collective-permute-start | bytes 589832 | tf_op jit(solution)/shard_map/ppermute | solution.py:494
  23.9 10.0 %collective-permute-start.3 = (f32[4,5,8,128]{3,2,1,0:T(8,128)S(1)}, f32[4,5,8,128]{3,2,1,0:T(8,128)S(1)}, u32[]{:S(2)}, u32[]{:S(2)}) collective-permute-start(f32[4,5,8,128]{3,2,1,0:T(8,128)S(1)} %get-tuple-element.29), channel_id=1, source_target_pairs={{0,2},{1,3},{2,0},{3,1},{4,6},{5,7},{6,4},{7,5},{8,10},{9,11},{10,... | collective-permute-start | bytes 245768 | tf_op jit(solution)/shard_map/ppermute | solution.py:509
  24.4 9.5 %collective-permute-start.4 = (f32[4,5,8,128]{3,2,1,0:T(8,128)S(1)}, f32[4,5,8,128]{3,2,1,0:T(8,128)S(1)}, u32[]{:S(2)}, u32[]{:S(2)}) collective-permute-start(f32[4,5,8,128]{3,2,1,0:T(8,128)S(1)} %get-tuple-element.30), channel_id=1, source_target_pairs={{0,3},{1,2},{2,1},{3,0},{4,7},{5,6},{6,5},{7,4},{8,11},{9,10},{10,... | collective-permute-start | bytes 245768 | tf_op jit(solution)/shard_map/ppermute | solution.py:509
  27.8 6.1 %collective-permute-start.5 = (f32[4,5,8,128]{3,2,1,0:T(8,128)S(1)}, f32[4,5,8,128]{3,2,1,0:T(8,128)S(1)}, u32[]{:S(2)}, u32[]{:S(2)}) collective-permute-start(f32[4,5,8,128]{3,2,1,0:T(8,128)S(1)} %get-tuple-element.31), channel_id=1, source_target_pairs={{0,1},{1,0},{2,3},{3,2},{4,5},{5,4},{6,7},{7,6},{8,9},{9,8},{10,11... | collective-permute-start | bytes 245768 | tf_op jit(solution)/shard_map/ppermute | solution.py:509
  29.7 5.8 %collective-permute-start.7 = (f32[4,3,8,128]{3,2,1,0:T(8,128)S(1)}, f32[4,3,8,128]{3,2,1,0:T(8,128)S(1)}, u32[]{:S(2)}, u32[]{:S(2)}) collective-permute-start(f32[4,3,8,128]{3,2,1,0:T(8,128)S(1)} %get-tuple-element.38), channel_id=1, source_target_pairs={{0,2},{1,3},{2,0},{3,1},{4,6},{5,7},{6,4},{7,5},{8,10},{9,11},{10,... | collective-permute-start | bytes 147464 | tf_op jit(solution)/shard_map/ppermute | solution.py:509
  30.4 6.3 %collective-permute-start.8 = (f32[4,3,8,128]{3,2,1,0:T(8,128)S(1)}, f32[4,3,8,128]{3,2,1,0:T(8,128)S(1)}, u32[]{:S(2)}, u32[]{:S(2)}) collective-permute-start(f32[4,3,8,128]{3,2,1,0:T(8,128)S(1)} %get-tuple-element.39), channel_id=1, source_target_pairs={{0,3},{1,2},{2,1},{3,0},{4,7},{5,6},{6,5},{7,4},{8,11},{9,10},{10,... | collective-permute-start | bytes 147464 | tf_op jit(solution)/shard_map/ppermute | solution.py:509
  33.9 2.8 %collective-permute-start.9 = (f32[4,3,8,128]{3,2,1,0:T(8,128)S(1)}, f32[4,3,8,128]{3,2,1,0:T(8,128)S(1)}, u32[]{:S(2)}, u32[]{:S(2)}) collective-permute-start(f32[4,3,8,128]{3,2,1,0:T(8,128)S(1)} %get-tuple-element.40), channel_id=1, source_target_pairs={{0,1},{1,0},{2,3},{3,2},{4,5},{5,4},{6,7},{7,6},{8,9},{9,8},{10,11... | collective-permute-start | bytes 147464 | tf_op jit(solution)/shard_map/ppermute | solution.py:509

commit v5 on v4

--- a/solution.py
+++ b/solution.py
@@ -45,7 +45,9 @@
         zhot[:, at] = place(row_iota[:128] == lane_of[a : a + 1])
 
 
-def nonlocal_rows(load_rows, orbs, index, projector, strength, parts, rowhot, zhot, picked, spread):
+def nonlocal_rows(
+    load_rows, beside, orbs, index, projector, strength, parts, rowhot, zhot, picked, spread
+):
     lanes = 128
     atoms, channels = projector.shape[0], projector.shape[1]
     for o in range(orbs):
@@ -57,6 +59,7 @@
     lane_iota = lax.broadcasted_iota(jnp.int32, (lanes, lanes), 0)
     for a in range(0, atoms, 2):
         at = slice(a * lanes, (a + 2) * lanes)
+        beside(a // 2, atoms // 2)
         found = jnp.dot(parts[0], rowhot[:, at], preferred_element_type=jnp.float32)
         found = found + jnp.dot(parts[1], rowhot[:, at], preferred_element_type=jnp.float32)
         for b in range(2):
@@ -119,8 +122,15 @@
     orbs, layers = v.shape[0], v.shape[1]
     slot_strengths(species, count, energy, strength)
     mark_cells(index, rowhot, zhot)
+
+    def local_terms(step, steps):
+        for n in range(step * orbs * layers // steps, (step + 1) * orbs * layers // steps):
+            o, i = divmod(n, layers)
+            out[o, i] = local_layer(lambda j: v[o, j], potential[i], i, layers)
+
     hat = nonlocal_rows(
         lambda o: v[o].reshape(256, 128),
+        local_terms,
         orbs,
         index,
         projector,
@@ -133,8 +143,7 @@
     )
     for o in range(orbs):
         for i in range(layers):
-            total = local_layer(lambda j: v[o, j], potential[i], i, layers)
-            total = total + hat[i * 16 : (i + 1) * 16, o * 128 : (o + 1) * 128]
+            total = out[o, i] + hat[i * 16 : (i + 1) * 16, o * 128 : (o + 1) * 128]
             out[o, i] = total * (1.0 / HALF_WIDTH)
     cut_edges(out, far, near)
 
@@ -165,8 +174,15 @@
         add_above(part.at[:, layers - RADIUS :], above, high, -0.5 / HALF_WIDTH)
 
     by_parity(edges, far, near)
+
+    def local_terms(step, steps):
+        for n in range(step * orbs * layers // steps, (step + 1) * orbs * layers // steps):
+            o, i = divmod(n, layers)
+            out[o, i] = local_layer(lambda j: held[o, j], potential[i], i, layers)
+
     hat = nonlocal_rows(
         lambda o: held[o].reshape(256, 128),
+        local_terms,
         orbs,
         index,
         projector,
@@ -179,8 +195,7 @@
     )
     for o in range(orbs):
         for i in range(layers):
-            total = local_layer(lambda j: held[o, j], potential[i], i, layers)
-            total = total + hat[i * 16 : (i + 1) * 16, o * 128 : (o + 1) * 128]
+            total = out[o, i] + hat[i * 16 : (i + 1) * 16, o * 128 : (o + 1) * 128]
             out[o, i] = total * (2.0 / HALF_WIDTH) - v[o, i]
 
 

time: 56.1 us -> 55.8 us (level)
  transfers between devices with their start and end apart: 10 -> 10, of which waited for: 3 -> 3; matrix products, arithmetic and copies ran while one was open for 0% -> 0% of each run, Pallas kernels for 17% -> 16%
where the time goes in v5:
time: 55.8 us; the launch traced here: 55.7 us
  starting transfers between devices  20.7 us (37%)
  blocking collectives  18 us (32%)
  Pallas kernels  10.5 us (19%)
  waiting for transfers between devices  3.86 us (7%)
  between operations  1.44 us (3%)
  local copies, waits for them, and re-layouts  1.14 us (2%)
    all_to_all x1, blocking collectives, on_device(): terms = lax.all_to_all(terms, ('dom', 'orb'), 0, 0)  18 us
    ppermute x1, starting transfers between devices, on_device(): got_far = lax.ppermute(far, 'dom', far_pairs)  9.74 us
    ppermute x6, starting transfers between devices, swap(): lax.ppermute(chunks[k], 'orb', [(i, i ^ k) for i in range(orb_devices)])  7.87 us
    pallas_call x1, Pallas kernels, on_device(): call(first_kernel, (edge, edge, block, jax.ShapeDtypeStruct((layers * wid...  3.9 us
    pallas_call x1, Pallas kernels, on_device(): call(second_kernel, block, [in_vmem] * 10, scratch + [pltpu.VMEM(orbitals...  3.33 us
    ppermute x1, starting transfers between devices, on_device(): got_near = lax.ppermute(near, 'dom', near_pairs)  2.13 us
    ppermute x1, waiting for transfers between devices, on_device(): next_far = lax.ppermute(far, 'dom', far_pairs)  1.79 us
    ppermute x6, waiting for transfers between devices, swap(): lax.ppermute(chunks[k], 'orb', [(i, i ^ k) for i in range(orb_devices)])  1.19 us
  transfers between devices with their start and end apart: 10, of which 3 were waited for; matrix products, arithmetic and copies ran while one was open for 0% of the time, Pallas kernels for 16%

profile of v5, /device:TPU:1, one launch (start us, length us, event | category | flops | bytes accessed | tf_op | source)
XLA Modules:
  0.0 55.7 jit_solution(13590947288801176342)
XLA Ops:
  0.6 1.1 %fusion = (f32[4,6,16,128]{3,2,1,0:T(8,128)S(1)}, f32[4,6,16,128]{3,2,1,0:T(8,128)S(1)}) fusion(f32[4,16,16,128]{3,2,1,0:T(8,128)} %v.7), kind=kLoop, calls=%fused_computation | loop fusion | bytes 786432 | tf_op jit(solution)/shard_map/slice | solution.py:486
  1.8 0.0 copy-start.1
  1.8 0.0 copy-start.2
  1.8 0.0 copy-start.3
  1.8 0.0 copy-start.4
  1.9 2.1 %collective-permute-start = (f32[4,6,16,128]{3,2,1,0:T(8,128)S(1)}, f32[4,6,16,128]{3,2,1,0:T(8,128)S(1)}, u32[]{:S(2)}, u32[]{:S(2)}) collective-permute-start(f32[4,6,16,128]{3,2,1,0:T(8,128)S(1)} %get-tuple-element.25), channel_id=1, source_target_pairs={{0,4},{4,0},{8,12},{12,8},{16,20},{20,16},{24,28},{28,24},{32,36},... | collective-permute-start | bytes 589832 | tf_op jit(solution)/shard_map/ppermute | solution.py:489
  4.0 9.7 %collective-permute-start.1 = (f32[4,6,16,128]{3,2,1,0:T(8,128)S(1)}, f32[4,6,16,128]{3,2,1,0:T(8,128)S(1)}, u32[]{:S(2)}, u32[]{:S(2)}) collective-permute-start(f32[4,6,16,128]{3,2,1,0:T(8,128)S(1)} %get-tuple-element.26), channel_id=1, source_target_pairs={{0,252},{4,8},{8,4},{12,16},{16,12},{20,24},{24,20},{28,32},{32,28... | collective-permute-start | bytes 589832 | tf_op jit(solution)/shard_map/ppermute | solution.py:488
  14.4 3.9 %shard_map.86 = (f32[4,6,16,128]{3,2,1,0:T(8,128)S(1)}, f32[4,6,16,128]{3,2,1,0:T(8,128)S(1)}, f32[4,16,16,128]{3,2,1,0:T(8,128)S(1)}, bf16[256,2048]{1,0:T(8,12...) custom-call(s32[16]{0:T(128)S(1)} %copy-done.5, s32[1]{0:T(128)S(6)} %copy.9.count, ...), custom_call_target="tpu_custom_call" | custom-call | flops 3000000000 | bytes 2097152 | tf_op jit(solution)/shard_map/pallas_call | solution.py:495
  18.3 0.1 collective-permute-start.2
  18.4 0.9 %collective-permute-start.6 = (f32[4,6,16,128]{3,2,1,0:T(8,128)S(1)}, f32[4,6,16,128]{3,2,1,0:T(8,128)S(1)}, u32[]{:S(2)}, u32[]{:S(2)}) collective-permute-start(f32[4,6,16,128]{3,2,1,0:T(8,128)S(1)} %get-tuple-element.34), channel_id=1, source_target_pairs={{0,252},{4,8},{8,4},{12,16},{16,12},{20,24},{24,20},{28,32},{32,28... | collective-permute-start | bytes 589832 | tf_op jit(solution)/shard_map/ppermute | solution.py:509
  19.4 0.0 collective-permute-done.near
  19.4 3.3 %shard_map.88.part = f32[4,16,16,128]{3,2,1,0:T(8,128)S(1)} custom-call(f32[4,16,16,128]{3,2,1,0:T(8,128)S(1)} %copy-done, f32[16,16,128]{2,1,0:T(8,128)S(1)} %copy-done.1, s32[16,128]{1,0:T(8,128)S(1)} %copy-done.3, f32[16,4,128]{2,1,0:T(4,128)S(1)} %copy-done.2, f32[4,16,128]{2,1,0:T(8,128)S(1)} %get-tuple-element.22.strength, ...), custom_call_target="tpu_custom_call" | custom-call | flops 3000000000 | bytes 2097152 | tf_op jit(solution)/shard_map/pallas_call | solution.py:511
  22.7 0.9 %collective-permute-done.2.got = f32[4,6,16,128]{3,2,1,0:T(8,128)S(1)} collective-permute-done((f32[4,6,16,128]{3,2,1,0:T(8,128)S(1)}, f32[4,6,16,128]{3,2,1,0:T(8,128)S(1)}, u32[]{:S(2)}, u32[]{:S(2)}) %collective-permute-start.2) | collective-permute-done | bytes 196640 | tf_op jit(solution)/shard_map/ppermute | solution.py:510
  23.6 0.1 shard_map.89
  23.7 0.5 collective-permute-start.3
  24.2 3.4 %collective-permute-start.4 = (f32[4,5,8,128]{3,2,1,0:T(8,128)S(1)}, f32[4,5,8,128]{3,2,1,0:T(8,128)S(1)}, u32[]{:S(2)}, u32[]{:S(2)}) collective-permute-start(f32[4,5,8,128]{3,2,1,0:T(8,128)S(1)} %get-tuple-element.30), channel_id=1, source_target_pairs={{0,3},{1,2},{2,1},{3,0},{4,7},{5,6},{6,5},{7,4},{8,11},{9,10},{10,... | collective-permute-start | bytes 245768 | tf_op jit(solution)/shard_map/ppermute | solution.py:524
  27.6 0.0 collective-permute-start.5
  27.6 1.8 %collective-permute-done.6.got = f32[4,6,16,128]{3,2,1,0:T(8,128)S(1)} collective-permute-done((f32[4,6,16,128]{3,2,1,0:T(8,128)S(1)}, f32[4,6,16,128]{3,2,1,0:T(8,128)S(1)}, u32[]{:S(2)}, u32[]{:S(2)}) %collective-permute-start.6) | collective-permute-done | bytes 196640 | tf_op jit(solution)/shard_map/ppermute | solution.py:509
  29.4 0.1 shard_map.91
  29.6 0.5 collective-permute-start.7
  30.0 3.5 %collective-permute-start.8 = (f32[4,3,8,128]{3,2,1,0:T(8,128)S(1)}, f32[4,3,8,128]{3,2,1,0:T(8,128)S(1)}, u32[]{:S(2)}, u32[]{:S(2)}) collective-permute-start(f32[4,3,8,128]{3,2,1,0:T(8,128)S(1)} %get-tuple-element.39), channel_id=1, source_target_pairs={{0,3},{1,2},{2,1},{3,0},{4,7},{5,6},{6,5},{7,4},{8,11},{9,10},{10,... | collective-permute-start | bytes 147464 | tf_op jit(solution)/shard_map/ppermute | solution.py:524
  33.5 0.0 collective-permute-done.3.got_2
  33.5 0.0 collective-permute-start.9
  33.6 0.0 collective-permute-done.5.got_1
  33.6 0.4 shard_map.90.early
  34.0 1.2 %shard_map.92 = (f32[4,16,16,128]{3,2,1,0:T(8,128)}, f32[1,128]{1,0:T(1,128)S(1)}) custom-call(f32[1,128]{1,0:T(1,128)S(1)} %shard_map.90.early, f32[4,20,8,128]{3,2,1,0:T(8,128)S(1)} %get-tuple-element.33.near, f32[4,12,8,128]{3,2,1,0:T(8,128)S(1)} %get-tuple-element.35.far), custom_call_target="tpu_custom_call" | custom-call | flops 1500000000 | bytes 2097152 | tf_op jit(solution)/shard_map/pallas_call | solution.py:548
  35.2 0.0 collective-permute-done.7.got_2
  35.2 1.2 %collective-permute-done.8.got_3 = f32[4,3,8,128]{3,2,1,0:T(8,128)S(1)} collective-permute-done((f32[4,3,8,128]{3,2,1,0:T(8,128)S(1)}, f32[4,3,8,128]{3,2,1,0:T(8,128)S(1)}, u32[]{:S(2)}, u32[]{:S(2)}) %collective-permute-start.8) | collective-permute-done | bytes 49184 | tf_op jit(solution)/shard_map/ppermute | solution.py:524
  36.4 0.0 collective-permute-done.9.got_1
  36.4 0.5 shard_map.93
  36.8 18.0 %all_to_all.5.terms = f32[256,1,128]{2,1,0:T(1,128)S(1)} all-to-all(f32[256,1,128]{2,1,0:T(1,128)S(1)} %shard_map.93), channel_id=1, replica_groups=mesh['dom'=64,'orb'=4] {'dom','orb'}, dimensions={0} | all-to-all | bytes 262144 | tf_op jit(solution)/shard_map/all_to_all | solution.py:557
  54.8 0.9 %shard_map.94 = f32[16,16]{1,0:T(8,128)} custom-call(f32[256,1,128]{2,1,0:T(1,128)S(1)} %all_to_all.5.terms), custom_call_target="tpu_custom_call" | custom-call | flops 10000000 | bytes 2097152 | tf_op jit(solution)/shard_map/pallas_call | solution.py:558
  (11 shorter events, 0.1 us)
Async XLA Ops:
  0.6 13.7 %copy-start = (f32[4,16,16,128]{3,2,1,0:T(8,128)S(1)}, f32[4,16,16,128]{3,2,1,0:T(8,128)}, u32[]{:S(2)}) copy-start(f32[4,16,16,128]{3,2,1,0:T(8,128)} %v.7) | copy-start | bytes 1572868
  1.8 12.6 %copy-start.1 = (f32[16,16,128]{2,1,0:T(8,128)S(1)}, f32[16,16,128]{2,1,0:T(8,128)}, u32[]{:S(2)}) copy-start(f32[16,16,128]{2,1,0:T(8,128)} %potential.3) | copy-start | bytes 393220
  1.8 12.6 %copy-start.2 = (f32[16,4,128]{2,1,0:T(4,128)S(1)}, f32[16,4,128]{2,1,0:T(4,128)}, u32[]{:S(2)}) copy-start(f32[16,4,128]{2,1,0:T(4,128)} %projector.3) | copy-start | bytes 98308
  1.8 12.6 %copy-start.3 = (s32[16,128]{1,0:T(8,128)S(1)}, s32[16,128]{1,0:T(8,128)}, u32[]{:S(2)}) copy-start(s32[16,128]{1,0:T(8,128)} %index.3) | copy-start | bytes 24580
  1.8 12.6 %copy-start.4 = (f32[3,4]{1,0:T(4,128)S(1)}, f32[3,4]{1,0:T(4,128)}, u32[]{:S(2)}) copy-start(f32[3,4]{1,0:T(4,128)} %energy.1) | copy-start | bytes 148
  1.9 17.5 %collective-permute-start = (f32[4,6,16,128]{3,2,1,0:T(8,128)S(1)}, f32[4,6,16,128]{3,2,1,0:T(8,128)S(1)}, u32[]{:S(2)}, u32[]{:S(2)}) collective-permute-start(f32[4,6,16,128]{3,2,1,0:T(8,128)S(1)} %get-tuple-element.25), channel_id=1, source_target_pairs={{0,4},{4,0},{8,12},{12,8},{16,20},{20,16},{24,28},{28,24},{32,36},... | collective-permute-start | bytes 589832 | tf_op jit(solution)/shard_map/ppermute | solution.py:489
  4.0 10.4 %copy-start.5 = (s32[16]{0:T(128)S(1)}, s32[16]{0:T(128)}, u32[]{:S(2)}) copy-start(s32[16]{0:T(128)} %species.1) | copy-start | bytes 196
  4.0 15.4 %collective-permute-start.1 = (f32[4,6,16,128]{3,2,1,0:T(8,128)S(1)}, f32[4,6,16,128]{3,2,1,0:T(8,128)S(1)}, u32[]{:S(2)}, u32[]{:S(2)}) collective-permute-start(f32[4,6,16,128]{3,2,1,0:T(8,128)S(1)} %get-tuple-element.26), channel_id=1, source_target_pairs={{0,252},{4,8},{8,4},{12,16},{16,12},{20,24},{24,20},{28,32},{32,28... | collective-permute-start | bytes 589832 | tf_op jit(solution)/shard_map/ppermute | solution.py:488
  18.3 5.2 %collective-permute-start.2 = (f32[4,6,16,128]{3,2,1,0:T(8,128)S(1)}, f32[4,6,16,128]{3,2,1,0:T(8,128)S(1)}, u32[]{:S(2)}, u32[]{:S(2)}) collective-permute-start(f32[4,6,16,128]{3,2,1,0:T(8,128)S(1)} %get-tuple-element.28), channel_id=1, source_target_pairs={{0,4},{4,0},{8,12},{12,8},{16,20},{20,16},{24,28},{28,24},{32,36},... | collective-permute-start | bytes 589832 | tf_op jit(solution)/shard_map/ppermute | solution.py:510
  18.4 11.0 %collective-permute-start.6 = (f32[4,6,16,128]{3,2,1,0:T(8,128)S(1)}, f32[4,6,16,128]{3,2,1,0:T(8,128)S(1)}, u32[]{:S(2)}, u32[]{:S(2)}) collective-permute-start(f32[4,6,16,128]{3,2,1,0:T(8,128)S(1)} %get-tuple-element.34), channel_id=1, source_target_pairs={{0,252},{4,8},{8,4},{12,16},{16,12},{20,24},{24,20},{28,32},{32,28... | collective-permute-start | bytes 589832 | tf_op jit(solution)/shard_map/ppermute | solution.py:509
  23.7 9.8 %collective-permute-start.3 = (f32[4,5,8,128]{3,2,1,0:T(8,128)S(1)}, f32[4,5,8,128]{3,2,1,0:T(8,128)S(1)}, u32[]{:S(2)}, u32[]{:S(2)}) collective-permute-start(f32[4,5,8,128]{3,2,1,0:T(8,128)S(1)} %get-tuple-element.29), channel_id=1, source_target_pairs={{0,2},{1,3},{2,0},{3,1},{4,6},{5,7},{6,4},{7,5},{8,10},{9,11},{10,... | collective-permute-start | bytes 245768 | tf_op jit(solution)/shard_map/ppermute | solution.py:524
  24.2 9.3 %collective-permute-start.4 = (f32[4,5,8,128]{3,2,1,0:T(8,128)S(1)}, f32[4,5,8,128]{3,2,1,0:T(8,128)S(1)}, u32[]{:S(2)}, u32[]{:S(2)}) collective-permute-start(f32[4,5,8,128]{3,2,1,0:T(8,128)S(1)} %get-tuple-element.30), channel_id=1, source_target_pairs={{0,3},{1,2},{2,1},{3,0},{4,7},{5,6},{6,5},{7,4},{8,11},{9,10},{10,... | collective-permute-start | bytes 245768 | tf_op jit(solution)/shard_map/ppermute | solution.py:524
  27.6 5.9 %collective-permute-start.5 = (f32[4,5,8,128]{3,2,1,0:T(8,128)S(1)}, f32[4,5,8,128]{3,2,1,0:T(8,128)S(1)}, u32[]{:S(2)}, u32[]{:S(2)}) collective-permute-start(f32[4,5,8,128]{3,2,1,0:T(8,128)S(1)} %get-tuple-element.31), channel_id=1, source_target_pairs={{0,1},{1,0},{2,3},{3,2},{4,5},{5,4},{6,7},{7,6},{8,9},{9,8},{10,11... | collective-permute-start | bytes 245768 | tf_op jit(solution)/shard_map/ppermute | solution.py:524
  29.6 5.6 %collective-permute-start.7 = (f32[4,3,8,128]{3,2,1,0:T(8,128)S(1)}, f32[4,3,8,128]{3,2,1,0:T(8,128)S(1)}, u32[]{:S(2)}, u32[]{:S(2)}) collective-permute-start(f32[4,3,8,128]{3,2,1,0:T(8,128)S(1)} %get-tuple-element.38), channel_id=1, source_target_pairs={{0,2},{1,3},{2,0},{3,1},{4,6},{5,7},{6,4},{7,5},{8,10},{9,11},{10,... | collective-permute-start | bytes 147464 | tf_op jit(solution)/shard_map/ppermute | solution.py:524
  30.0 6.3 %collective-permute-start.8 = (f32[4,3,8,128]{3,2,1,0:T(8,128)S(1)}, f32[4,3,8,128]{3,2,1,0:T(8,128)S(1)}, u32[]{:S(2)}, u32[]{:S(2)}) collective-permute-start(f32[4,3,8,128]{3,2,1,0:T(8,128)S(1)} %get-tuple-element.39), channel_id=1, source_target_pairs={{0,3},{1,2},{2,1},{3,0},{4,7},{5,6},{6,5},{7,4},{8,11},{9,10},{10,... | collective-permute-start | bytes 147464 | tf_op jit(solution)/shard_map/ppermute | solution.py:524
  33.5 2.8 %collective-permute-start.9 = (f32[4,3,8,128]{3,2,1,0:T(8,128)S(1)}, f32[4,3,8,128]{3,2,1,0:T(8,128)S(1)}, u32[]{:S(2)}, u32[]{:S(2)}) collective-permute-start(f32[4,3,8,128]{3,2,1,0:T(8,128)S(1)} %get-tuple-element.40), channel_id=1, source_target_pairs={{0,1},{1,0},{2,3},{3,2},{4,5},{5,4},{6,7},{7,6},{8,9},{9,8},{10,11... | collective-permute-start | bytes 147464 | tf_op jit(solution)/shard_map/ppermute | solution.py:524
